TPU v7x, 512 devices: a whole 4x4x16 slice. The times are simulated.
512 devices in a mesh: coef: 32 (over z, x_lo), band: 16 (over x_hi, y, core).
Axes of the slice: x: 4 (x_hi: 2, x_lo: 2; x = x_hi * 2 + x_lo), y: 4, z: 16, core: 2. Of those that a mesh axis runs over, the one named last changes fastest.
Arguments:
- wave: bfloat16 [4096, 131072], P('band', 'coef')
- projector: bfloat16 [512, 131072], P('band', 'coef'), may hold values from -0.015625 to 0.015625
- gvec: int32 [3, 131072], P(None, 'coef'), may hold values from -13 to 13, as said below
- atom_of: int32 [512], replicated, may hold values from 0 to 63, never falling along the last dimension, each value on 1 to 16 neighbouring positions
- dion: bfloat16 [512, 512], replicated
- qaug: bfloat16 [512, 512], replicated, as said below
Outputs:
- precond_resid: bfloat16 [4096, 131072], P('band', 'coef')
Inputs may be any that keep to these rules, and one draw needn't show every extreme that they name: `gvec`: no component is zero. `qaug`: within any set of at most 16 projectors, each diagonal entry exceeds both the sum of magnitudes of the other entries of its row and that of its column in that set.
All inputs are finite; a program needn't handle non-finite values.
Results may differ from a plain program's by a relative error of at most 0.0047.
Values may be sent and summed in bfloat16 or wider, within the bound.
No kernel may reach another device: no remote copies, remote signals or barrier semaphores. Data moves between devices by JAX's collectives and lax.ppermute only.
A program may use at most 64 MiB of HBM per device.

v0:
```python
import jax
import jax.numpy as jnp
from jax import lax
from jax.sharding import PartitionSpec as P

kinetic_unit = 0.005


def kinetic(gvec):
    comps = gvec.astype(jnp.float32)
    return kinetic_unit * jnp.sum(comps * comps, axis=0)


def masked(atom_of, dion, qaug):
    same = atom_of[:, None] == atom_of[None, :]
    dmask = jnp.where(same, dion.astype(jnp.float32), jnp.float32(0.0))
    qmask = jnp.where(same, qaug.astype(jnp.float32), jnp.float32(0.0))
    return (dmask, qmask)


def couple(intersection, sq, ksq, dmask, qmask):
    pd = jnp.dot(intersection, dmask, precision=lax.Precision.HIGHEST)
    pq = jnp.dot(intersection, qmask, precision=lax.Precision.HIGHEST)
    energy = (ksq + jnp.sum(intersection * pd, axis=1)) / (sq + jnp.sum(intersection * pq, axis=1))
    ekin = ksq / (sq + 1e-06)
    coupled = (pd - energy[:, None] * pq).astype(jnp.bfloat16)
    return (coupled, energy, ekin)


def finish(wave, kin, expanded, energy, ekin):
    wavef = wave.astype(jnp.float32)
    resid = (kin[None, :] - energy[:, None]) * wavef + expanded
    ratio = kin[None, :] / ekin[:, None]
    num = 27.0 + ratio * (18.0 + ratio * (12.0 + 8.0 * ratio))
    return (num / (num + 16.0 * ratio**4) * resid).astype(jnp.bfloat16)


def against(left, right):
    return lax.dot_general(
        left, right, (((1,), (1,)), ((), ())), preferred_element_type=jnp.float32
    )


def on_device(wave, projector, gvec, atom_of, dion, qaug):
    kin = kinetic(gvec)
    dmask, qmask = masked(atom_of, dion, qaug)
    wavef = wave.astype(jnp.float32)
    sq = jnp.sum(wavef * wavef, axis=1)
    ksq = jnp.sum(kin[None, :] * wavef * wavef, axis=1)
    gathered = lax.all_gather(projector, "band", axis=0, tiled=True)
    partial_value = against(wave, gathered)
    sq, ksq = lax.psum((sq, ksq), "coef")
    intersection = lax.psum(partial_value, "coef")
    coupled, energy, ekin = couple(intersection, sq, ksq, dmask, qmask)
    expanded = jnp.dot(coupled, gathered, preferred_element_type=jnp.float32)
    return finish(wave, kin, expanded, energy, ekin)


def solution(mesh):
    in_specs = (P("band", "coef"), P("band", "coef"), P(None, "coef"), P(), P(), P())
    out_specs = P("band", "coef")
    return jax.shard_map(
        on_device, mesh=mesh, in_specs=in_specs, out_specs=out_specs, check_vma=False
    )
```

profile of v0, /device:TPU:6, one launch (start us, length us, event | category | flops | bytes accessed | tf_op | source)
XLA Modules:
  0.0 370.2 jit_solution(17010006491379212380)
XLA Ops:
  6.5 0.0 all-gather.2.cloned.1.call-start
  6.5 0.7 all-gather.2.cloned.1.call-update
  7.3 0.0 copy-start
  7.3 0.0 all-reduce.3.cloned.1.call-start
  7.3 1.0 multiply_reduce_fusion.2
  8.3 0.0 copy-start.1
  8.4 0.0 copy-start.3
  8.4 0.0 copy-start.2
  8.4 75.8 %all-gather.2.cloned.1.call-done = bf16[512,4096]{1,0:T(8,128)(2,1)} async-done(((bf16[32,4096]{1,0:T(8,128)(2,1)}), bf16[512,4096]{1,0:T(8,128)(2,1)}) %all-gather.2.cloned.1.call-update) | async-done | bytes 4194320 | tf_op jit(solution)/shard_map/all_gather | solution.py:50
  84.2 4.9 %fusion.17 = f32[256,512]{1,0:T(8,128)} fusion(bf16[256,4096]{1,0:T(8,128)(2,1)} %param.6, bf16[512,4096]{1,0:T(8,128)(2,1)} %all-gather.2.cloned.1.call-done), kind=kOutput, calls=%fused_computation.32 | convolution fusion | flops 1073741824 | bytes 6815744 | tf_op jit(solution)/shard_map/dot_general | solution.py:39
  89.1 0.0 all-reduce.3.cloned.1.call-update
  89.1 0.0 copy-done
  89.2 0.9 fusion.2
  90.1 61.3 %all-reduce = (f32[256]{0:T(256)S(1)}, f32[256]{0:T(256)S(1)}) all-reduce(f32[256]{0:T(256)S(1)} %get-tuple-element.6, f32[256]{0:T(256)S(1)} %get-tuple-element.5), channel_id=1, replica_groups=mesh['coef'=32,'band'=16] {'coef'}, use_global_device_ids=true, to_apply=%region_4.5 | all-reduce | flops 512 | bytes 4096 | tf_op jit(solution)/shard_map/psum | solution.py:52
  151.4 199.8 %all-reduce.3.cloned.1.call-done = f32[256,512]{1,0:T(8,128)} async-done(((f32[256,512]{1,0:T(8,128)}), f32[256,512]{1,0:T(8,128)}) %all-reduce.3.cloned.1.call-update) | async-done | bytes 524304 | tf_op jit(solution)/shard_map/psum | solution.py:53
  351.2 0.0 copy-done.1
  351.2 0.0 copy-done.3
  351.2 2.3 fusion.5
  353.5 0.0 copy-done.2
  353.5 2.6 multiply_reduce_fusion.1
  356.1 7.3 %fusion.1 = bf16[256,4096]{1,0:T(8,128)(2,1)} fusion(bf16[512,4096]{1,0:T(8,128)(2,1)} %all-gather.2.cloned.1.call-done, bf16[256,4096]{1,0:T(8,128)(2,1)S(1)} %copy-done, f32[256]{0:T(256)S(1)} %get-tuple-element.12, f32[256]{0:T(256)S(1)} %get-tuple-element.11, f32[4096]{0:T(1024)S(1)} %broadcast_multiply_fusion, f32[256,512]{1,0:T(8,128)S(1)} %get-tuple-element.13, ...), kind=kOutput, calls=%fused_computation.7 | convolution fusion | flops 1093009408 | bytes 9455616 | tf_op jit(solution)/shard_map/dot_general | solution.py:55
  (2 shorter events, 0.0 us)
Async XLA Ops:
  6.5 77.7 %all-gather.2.cloned.1.call-start = ((), (), s32[]{:S(2)}) async-start(), calls=%async_computation | async-start | bytes 4456448 | tf_op jit(solution)/shard_map/all_gather | solution.py:50
  7.3 81.9 %copy-start = (bf16[256,4096]{1,0:T(8,128)(2,1)S(1)}, bf16[256,4096]{1,0:T(8,128)(2,1)}, u32[]{:S(2)}) copy-start(bf16[256,4096]{1,0:T(8,128)(2,1)} %param.6) | copy-start | bytes 6291460
  7.3 343.9 %all-reduce.3.cloned.1.call-start = ((), (), s32[]{:S(2)}) async-start(), calls=%async_computation.1 | async-start | bytes 1048576 | tf_op jit(solution)/shard_map/psum | solution.py:53
  8.3 342.9 %copy-start.1 = (bf16[512,512]{1,0:T(8,128)(2,1)S(1)}, bf16[512,512]{1,0:T(8,128)(2,1)}, u32[]{:S(2)}) copy-start(bf16[512,512]{1,0:T(8,128)(2,1)} %param.11) | copy-start | bytes 1572868
  8.4 342.9 %copy-start.3 = (s32[512]{0:T(512)S(1)}, s32[512]{0:T(512)}, u32[]{:S(2)}) copy-start(s32[512]{0:T(512)} %param.9) | copy-start | bytes 6148
  8.4 345.1 %copy-start.2 = (bf16[512,512]{1,0:T(8,128)(2,1)S(1)}, bf16[512,512]{1,0:T(8,128)(2,1)}, u32[]{:S(2)}) copy-start(bf16[512,512]{1,0:T(8,128)(2,1)} %param.10) | copy-start | bytes 1572868
Sparse Core Ops, SparseCore 0:
  10.7 73.4 all-gather.1
  89.3 261.9 all-reduce.2
where the time goes:
time: 371 us; the launch traced here: 370 us
  waiting for transfers between devices  276 us (74%)
  blocking collectives  61.3 us (17%)
  matrix products  17 us (5%)
  between operations  13.5 us (4%)
    psum x1, waiting for transfers between devices, on_device(): intersection = lax.psum(partial_value, 'coef')  200 us
    all_gather x1, waiting for transfers between devices, on_device(): gathered = lax.all_gather(projector, 'band', axis=0, tiled=True)  75.8 us
    psum x1, blocking collectives, on_device(): sq, ksq = lax.psum((sq, ksq), 'coef')  61.3 us
  transfers between devices with their start and end apart: 2, of which 2 were waited for; matrix products, arithmetic and copies ran while one was open for 1% of the time, Pallas kernels for 0%

commit v1 on v0

v1 whole, which is shorter than its diff:
```python
import functools
import jax
import jax.numpy as jnp
from jax import lax
from jax.experimental import pallas as pl
from jax.experimental.pallas import tpu as pltpu
from jax.sharding import PartitionSpec as P

kinetic_unit = 0.005
f32 = jnp.float32
bf16 = jnp.bfloat16

N_COEF = 32
N_BAND = 16
ROWS = 256
COLS = 4096
NPROJ = 512
SHARD = NPROJ // N_BAND
HALF_PROJ = NPROJ // 2
QUARTER_PROJ = NPROJ // 4
NEAR = 8
BANDS = ROWS // NEAR
STAT_ROWS = BANDS // 4
NEAR_ROWS = 2 * BANDS + STAT_ROWS
FAR_ROWS = BANDS + STAT_ROWS
N_Z_HI = N_COEF // NEAR
FAR = 2 * N_Z_HI

anywhere = pl.BlockSpec(memory_space=pl.ANY)
vmem = pl.BlockSpec(memory_space=pltpu.VMEM)
smem = pl.BlockSpec(memory_space=pltpu.SMEM)

CORE, Z_HI, ORDER = 0, 1, 2


def in_vmem(value):
    return pltpu.with_memory_space_constraint(value, pltpu.VMEM)


def in_hbm(value):
    return pltpu.with_memory_space_constraint(value, pltpu.HBM)


def params(mib):
    return pltpu.CompilerParams(vmem_limit_bytes=mib * 1024 * 1024)


def cost(flops, bytes_accessed):
    return pl.CostEstimate(flops=flops, bytes_accessed=bytes_accessed, transcendentals=0)


def pieces(value):
    hi = value.astype(bf16).astype(f32)
    rest = value - hi
    mid = rest.astype(bf16).astype(f32)
    lo = (rest - mid).astype(bf16).astype(f32)
    return hi, mid, lo


def stat_lanes():
    return lax.broadcasted_iota(jnp.int32, (STAT_ROWS, HALF_PROJ), 1)


def split_rows(value):
    lane = stat_lanes() & 63
    hi, mid, lo = [jnp.where((lane == 0) | (lane == 3), piece, 0.0) for piece in pieces(value)]
    return hi + pltpu.roll(mid, 1, 1) + pltpu.roll(lo, 2, 1)


def join_rows(packed):
    return packed + pltpu.roll(packed, HALF_PROJ - 1, 1) + pltpu.roll(packed, HALF_PROJ - 2, 1)


def to_rows(first, second):
    lane = stat_lanes()
    out = jnp.zeros((STAT_ROWS, HALF_PROJ), f32)
    for k in range(4):
        rows = slice(k * STAT_ROWS, (k + 1) * STAT_ROWS)
        out = jnp.where(lane == 64 * k, first[rows], jnp.where(lane == 64 * k + 3, second[rows], out))
    return split_rows(out)


def from_rows(packed):
    lane = stat_lanes()
    columns = []
    for begin in (0, 3):
        columns.append(jnp.concatenate([
            jnp.sum(jnp.where((lane >= 64 * k + begin) & (lane < 64 * k + begin + 3), packed, 0.0), axis=1, keepdims=True)
            for k in range(4)
        ], axis=0))
    return columns


def kinetic(gvec):
    comps = gvec.astype(f32)
    return kinetic_unit * (comps[0:1] * comps[0:1] + comps[1:2] * comps[1:2] + comps[2:3] * comps[2:3])


def stats_kernel(wave, gvec, stat, wave_v, sems):
    copies = [
        pltpu.make_async_copy(
            wave.at[pl.ds(n * BANDS, BANDS), :], wave_v.at[pl.ds(n * BANDS, BANDS), :], sems.at[n])
        for n in range(NEAR)
    ]
    for copy in copies:
        copy.start()
    kin = kinetic(gvec[...])
    for n, copy in enumerate(copies):
        copy.wait()
        value = wave_v[n * BANDS:(n + 1) * BANDS, :].astype(f32)
        square = value * value
        sq = jnp.sum(square, axis=1, keepdims=True)
        ksq = jnp.sum(square * kin, axis=1, keepdims=True)
        stat[n * STAT_ROWS:(n + 1) * STAT_ROWS, :] = to_rows(sq, ksq)


def stats(wave, gvec):
    return pl.pallas_call(
        stats_kernel,
        in_specs=[anywhere, vmem],
        out_specs=[vmem, vmem],
        out_shape=[
            jax.ShapeDtypeStruct((NEAR * STAT_ROWS, HALF_PROJ), f32),
            pltpu.VMEM((ROWS, COLS), bf16),
        ],
        scratch_shapes=[pltpu.SemaphoreType.DMA((NEAR,))],
        compiler_params=params(16),
        cost_estimate=cost(5 * ROWS * COLS, 2 * ROWS * COLS),
        name="stats",
    )(in_hbm(wave), gvec)


def weights_kernel(atom_of, dion, qaug, out):
    number = lax.broadcasted_iota(jnp.int32, (64, NPROJ), 0)
    member = jnp.where(atom_of[...] == number, 1.0, 0.0).astype(bf16)
    same = lax.dot_general(member, member, (((0,), (0,)), ((), ())), preferred_element_type=f32) > 0.5
    to = lax.broadcasted_iota(jnp.int32, (NPROJ, NPROJ), 0)
    source = ((to & 0xE0) << 1) | ((to >> 8) << 5) | (to & 31)
    order = jnp.where(source == lax.broadcasted_iota(jnp.int32, (NPROJ, NPROJ), 1), 1.0, 0.0).astype(bf16)
    for at, matrix in enumerate((dion, qaug)):
        value = jnp.where(same, matrix[...].astype(f32), 0.0).astype(bf16)
        rows = jnp.dot(order, value, preferred_element_type=f32).astype(bf16)
        out[:, at * NPROJ:(at + 1) * NPROJ] = lax.dot_general(
            rows, order, (((1,), (1,)), ((), ())), preferred_element_type=f32).astype(bf16)


def masked_weights(atom_of, dion, qaug):
    return pl.pallas_call(
        weights_kernel,
        in_specs=[vmem] * 3,
        out_specs=vmem,
        out_shape=jax.ShapeDtypeStruct((NPROJ, 2 * NPROJ), bf16),
        compiler_params=params(24),
        cost_estimate=cost(9 * NPROJ ** 3, 8 * NPROJ * NPROJ),
        name="masked_weights",
    )(atom_of.reshape(1, NPROJ), dion, qaug)


def against(left, right):
    return lax.dot_general(left, right, (((1,), (1,)), ((), ())), preferred_element_type=f32)


N_SHARDS = HALF_PROJ // SHARD


def intersect_kernel(place, stat, wave_own, wave_other, *refs):
    shards = refs[:N_SHARDS]
    message, whole, whole_v, message_v, out_sem = refs[N_SHARDS:]
    for i, shard in enumerate(shards):
        at = pl.multiple_of(place[ORDER + i] * SHARD, SHARD)
        whole_v[pl.ds(at, SHARD), :] = shard[...]
    back = pltpu.make_async_copy(whole_v, whole, out_sem)
    back.start()
    for core, wave in enumerate((wave_own, wave_other)):
        total = against(wave[...], whole_v[...])
        for n in range(NEAR):
            at = n * NEAR_ROWS + core * BANDS
            message_v[at:at + BANDS, :] = total[n * BANDS:(n + 1) * BANDS]
    for n in range(NEAR):
        at = n * NEAR_ROWS + 2 * BANDS
        message_v[at:at + STAT_ROWS, :] = stat[n * STAT_ROWS:(n + 1) * STAT_ROWS, :]
    message[...] = message_v[...].astype(bf16)
    back.wait()


def intersect(place, stat, wave_own, wave_other, shards):
    return pl.pallas_call(
        intersect_kernel,
        in_specs=[smem] + [vmem] * (3 + N_SHARDS),
        out_specs=[vmem, anywhere],
        out_shape=[
            jax.ShapeDtypeStruct((NEAR * NEAR_ROWS, HALF_PROJ), bf16),
            pltpu.HBM((HALF_PROJ, COLS), bf16),
        ],
        scratch_shapes=[
            pltpu.VMEM((HALF_PROJ, COLS), bf16),
            pltpu.VMEM((NEAR * NEAR_ROWS, HALF_PROJ), f32),
            pltpu.SemaphoreType.DMA,
        ],
        compiler_params=params(24),
        cost_estimate=cost(4 * ROWS * COLS * HALF_PROJ, 2 * (2 * ROWS + 2 * HALF_PROJ) * COLS),
        name="intersect",
    )(place, stat, in_vmem(wave_own), in_vmem(wave_other), *[in_vmem(shard) for shard in shards])


def near_sum_kernel(place, received, keep, message, message_v):
    total = jnp.sum(received[...].astype(f32).reshape(NEAR, NEAR_ROWS, HALF_PROJ), axis=0)
    keep[...] = total[:BANDS]
    rows = split_rows(join_rows(total[2 * BANDS:]))
    core = place[CORE]
    for zh in range(N_Z_HI):
        for c, value in ((core, total[:BANDS]), (1 - core, total[BANDS:2 * BANDS])):
            at = pl.multiple_of((zh * 2 + c) * FAR_ROWS, STAT_ROWS)
            message_v[pl.ds(at, BANDS), :] = value
            message_v[pl.ds(at + BANDS, STAT_ROWS), :] = rows
    message[...] = message_v[...].astype(bf16)


def near_sum(place, received):
    return pl.pallas_call(
        near_sum_kernel,
        in_specs=[smem, vmem],
        out_specs=[vmem, vmem],
        out_shape=[
            jax.ShapeDtypeStruct((BANDS, HALF_PROJ), f32),
            jax.ShapeDtypeStruct((FAR * FAR_ROWS, HALF_PROJ), bf16),
        ],
        scratch_shapes=[pltpu.VMEM((FAR * FAR_ROWS, HALF_PROJ), f32)],
        compiler_params=params(16),
        cost_estimate=cost(NEAR * NEAR_ROWS * HALF_PROJ, 3 * NEAR * NEAR_ROWS * HALF_PROJ),
        name="near_sum",
    )(place, received)


def couple_kernel(place, keep, received, weights, out):
    blocks = received[...].astype(f32).reshape(FAR, FAR_ROWS, HALF_PROJ)
    core = place[CORE]
    own_at = place[Z_HI] * 2 + core
    halves, packed = [], []
    for c in range(2):
        total = jnp.zeros((BANDS, HALF_PROJ), f32)
        rows = jnp.zeros((STAT_ROWS, HALF_PROJ), f32)
        for zh in range(N_Z_HI):
            block = blocks[zh * 2 + c]
            total += jnp.where(own_at == zh * 2 + c, keep[...], block[:BANDS])
            rows += block[BANDS:]
        halves.append(total)
        packed.append(rows)
    inter = jnp.concatenate(halves, axis=1)
    sq, ksq = from_rows(jnp.where(core == 0, packed[0], packed[1]))
    stacked = jnp.concatenate(pieces(inter), axis=0).astype(bf16)
    both = jnp.dot(stacked, weights[...], preferred_element_type=f32)
    both = both[:BANDS] + (both[BANDS:2 * BANDS] + both[2 * BANDS:])
    pd, pq = both[:, :NPROJ], both[:, NPROJ:]
    energy = (ksq + jnp.sum(inter * pd, axis=1, keepdims=True)) / (
        sq + jnp.sum(inter * pq, axis=1, keepdims=True))
    ekin = ksq / (sq + 1e-6)
    coupled = pd - energy * pq
    block = jnp.concatenate([coupled[:, :HALF_PROJ], coupled[:, HALF_PROJ:], to_rows(energy, ekin)], axis=0)
    out[...] = jnp.concatenate([block] * NEAR, axis=0).astype(bf16)


def couple(place, keep, received, weights):
    return pl.pallas_call(
        couple_kernel,
        in_specs=[smem] + [vmem] * 3,
        out_specs=vmem,
        out_shape=jax.ShapeDtypeStruct((NEAR * NEAR_ROWS, HALF_PROJ), bf16),
        compiler_params=params(16),
        cost_estimate=cost(12 * BANDS * NPROJ * NPROJ, 4 * NPROJ * NPROJ + 4 * ROWS * NPROJ),
        name="couple",
    )(place, keep, received, weights)


TILE = 256
N_TILES = COLS // TILE
CHUNK = 16


def finish_kernel(place, coupled, gvec, wave, whole_own, whole_other, out,
                  own_v, other_v, out_v, halves_v, energy_v, scale_v, even_v, odd_v, sems, out_sems):
    def columns(tile):
        return pl.ds(pl.multiple_of(tile * TILE, TILE), TILE)

    def copies(tile):
        cols = columns(tile)
        return [
            pltpu.make_async_copy(whole_own.at[:, cols], own_v.at[:, cols], sems.at[tile, 0]),
            pltpu.make_async_copy(whole_other.at[:, cols], other_v.at[:, cols], sems.at[tile, 1]),
        ]

    def out_copy(tile):
        cols = columns(tile)
        return pltpu.make_async_copy(out_v.at[:, cols], out.at[:, cols], out_sems.at[tile])

    def arrive(tile):
        for copy in copies(tile):
            copy.wait()

    def expand(tile, expanded_v):
        cols = columns(tile)
        expanded_v[...] = jnp.dot(halves_v[:ROWS, :], own_v[:, cols], preferred_element_type=f32) + jnp.dot(
            halves_v[ROWS:, :], other_v[:, cols], preferred_element_type=f32)

    def conclude(tile, expanded_v):
        cols = columns(tile)
        kin = jnp.broadcast_to(kinetic(gvec[:, cols]), (CHUNK, TILE))
        for i in range(ROWS // CHUNK):
            rows = slice(i * CHUNK, (i + 1) * CHUNK)
            energy = jnp.concatenate([energy_v[rows, :]] * (TILE // 128), axis=1)
            scale = jnp.concatenate([scale_v[rows, :]] * (TILE // 128), axis=1)
            resid = (kin - energy) * wave[rows, cols].astype(f32) + expanded_v[rows, :]
            u = kin * scale
            v = u * u
            num = (1.0 + u) * (1.0 + v)
            inverse = pl.reciprocal(num + 3.0 * (v * v), approx=True)
            out_v[rows, cols] = ((num * inverse) * resid).astype(bf16)

    for tile in range(N_TILES):
        for copy in copies(tile):
            copy.start()
    core = place[CORE]
    blocks = coupled[...].astype(f32).reshape(NEAR, NEAR_ROWS, HALF_PROJ)
    for n in range(NEAR):
        rows = slice(n * BANDS, (n + 1) * BANDS)
        first, second = blocks[n, :BANDS].astype(bf16), blocks[n, BANDS:2 * BANDS].astype(bf16)
        halves_v[rows, :] = jnp.where(core == 0, first, second)
        halves_v[ROWS + n * BANDS:ROWS + (n + 1) * BANDS, :] = jnp.where(core == 0, second, first)
        energy, ekin = from_rows(blocks[n, 2 * BANDS:])
        energy_v[rows, :] = jnp.broadcast_to(energy, (BANDS, 128))
        scale_v[rows, :] = jnp.broadcast_to((2.0 / 3.0) / ekin, (BANDS, 128))
    arrive(0)
    expand(0, even_v)

    @pl.loop(0, N_TILES // 2)
    def _(i):
        arrive(2 * i + 1)

        @pl.when(i + 1 < N_TILES // 2)
        def _():
            arrive(2 * i + 2)

        expand(2 * i + 1, odd_v)
        conclude(2 * i, even_v)
        out_copy(2 * i).start()
        expand(jnp.minimum(2 * i + 2, N_TILES - 1), even_v)
        conclude(2 * i + 1, odd_v)
        out_copy(2 * i + 1).start()

    for tile in range(N_TILES):
        out_copy(tile).wait()


def finish(place, coupled, wave, gvec, whole_own, whole_other):
    return pl.pallas_call(
        finish_kernel,
        in_specs=[smem] + [vmem] * 3 + [anywhere] * 2,
        out_specs=anywhere,
        out_shape=jax.ShapeDtypeStruct((ROWS, COLS), bf16),
        scratch_shapes=[pltpu.VMEM((HALF_PROJ, COLS), bf16)] * 2
        + [pltpu.VMEM((ROWS, COLS), bf16), pltpu.VMEM((2 * ROWS, HALF_PROJ), bf16)]
        + [pltpu.VMEM((ROWS, 128), f32)] * 2 + [pltpu.VMEM((ROWS, TILE), f32)] * 2
        + [pltpu.SemaphoreType.DMA((N_TILES, 2)), pltpu.SemaphoreType.DMA((N_TILES,))],
        compiler_params=params(24),
        cost_estimate=cost(2 * ROWS * COLS * NPROJ, 2 * (2 * ROWS + NPROJ) * COLS),
        name="finish",
    )(place, coupled, gvec, in_vmem(wave), in_hbm(whole_own), whole_other)


def band_perm(move):
    pairs = []
    for b in range(N_BAND):
        x, y, c = move(b // 8, (b // 2) % 4, b % 2)
        pairs.append((b, (x % 2) * 8 + (y % 4) * 2 + c))
    return pairs


def along_band(value, move):
    return lax.ppermute(value, "band", band_perm(move))


def swap(value):
    return along_band(value, lambda x, y, c: (x, y, 1 - c))


def ring(value):
    return along_band(value, lambda x, y, c: (x, y + 1 - 2 * c, c))


def against_ring(value):
    return along_band(value, lambda x, y, c: (x, y - 1 + 2 * c, c))


def to_other_x(value):
    return along_band(value, lambda x, y, c: (x + 1, y, c))


def near_exchange(value):
    groups = [[zh * NEAR + n for n in range(NEAR)] for zh in range(N_Z_HI)]
    return lax.all_to_all(value, "coef", 0, 0, axis_index_groups=groups, tiled=True)


def far_exchange(value):
    groups = [
        [(zh * NEAR + n) * N_BAND + chip * 2 + core for zh in range(N_Z_HI) for core in range(2)]
        for n in range(NEAR) for chip in range(N_BAND // 2)
    ]
    return lax.all_to_all(value, ("coef", "band"), 0, 0, axis_index_groups=groups, tiled=True)


def on_device(wave, projector, gvec, atom_of, dion, qaug):
    b, c = lax.axis_index("band"), lax.axis_index("coef")
    x, y, core, z_hi = b >> 3, (b >> 1) & 3, b & 1, c >> 3
    order = [y, (y + 3 + 2 * core) & 3, (y + 1 + 2 * core) & 3, (y + 2) & 3]
    place = jnp.stack(
        [core, z_hi] + [x * 4 + at for at in order] + [(1 - x) * 4 + at for at in order]).astype(jnp.int32)

    across = to_other_x(projector)
    before, after = ring(projector), against_ring(projector)
    far = ring(before)
    stat, wave_v = stats(wave, gvec)
    across, after, far, own_wave, stat = lax.optimization_barrier((across, after, far, wave, stat))
    far_x = to_other_x(far)
    before_x, after_x = ring(across), against_ring(across)
    wave_other = swap(own_wave)
    shards = [projector, before, after, far, across, before_x, after_x, far_x]
    message, whole = intersect(place, stat, wave_v, wave_other, shards)
    message, dion = lax.optimization_barrier((message, dion))
    weights = masked_weights(atom_of, dion, qaug)

    received, weights = lax.optimization_barrier((near_exchange(message), weights))
    keep, message = near_sum(place, received)
    coupled = near_exchange(couple(place, keep, far_exchange(message), weights))
    return finish(place, coupled, wave_v, gvec, whole, swap(whole))


def solution(mesh):
    in_specs = (P("band", "coef"), P("band", "coef"), P(None, "coef"), P(), P(), P())
    out_specs = P("band", "coef")
    return jax.shard_map(
        on_device, mesh=mesh, in_specs=in_specs, out_specs=out_specs, check_vma=False
    )
```

time: 371 us -> 110 us (0.30)
  waiting for transfers between devices: 276 us -> 21.6 us
  starting transfers between devices: 0.04 us -> 39.3 us
  blocking collectives: 61.3 us -> 27.5 us
  Pallas kernels: 0 us -> 17.4 us
  matrix products: 17 us -> 0 us
  between operations: 13.5 us -> 0.18 us
    psum x1 -> x0, waiting for transfers between devices: 200 us -> none  [on_device(): intersection = lax.psum(partial_value, 'coef')]
    all_gather x1 -> x0, waiting for transfers between devices: 75.8 us -> none  [on_device(): gathered = lax.all_gather(projector, 'band', axis=0, tiled=True)]
    psum x1 -> x0, blocking collectives: 61.3 us -> none  [on_device(): sq, ksq = lax.psum((sq, ksq), 'coef')]
    all_to_all x0 -> x1, blocking collectives: none -> 27.5 us  [far_exchange(): lax.all_to_all(value, ('coef', 'band'), 0, 0, axis_index_groups=groups, t...]
    ppermute x0 -> x9, starting transfers between devices: none -> 26.7 us  [along_band(): return lax.ppermute(value, 'band', band_perm(move))]
    pallas_call x0 -> x6, Pallas kernels: none -> 17.4 us  [the longest x1 6.38 us: finish(): pl.pallas_call(finish_kernel, in_specs=[smem] + [vmem] * 3 + [anywhere] *...]
    dot_general x4 -> x0, matrix products: 17 us -> none  [the longest x1 7.28 us: on_device(): expanded = jnp.dot(coupled, gathered, preferred_element_type=jnp.float32)]
    all_to_all x0 -> x2, starting transfers between devices: none -> 12.7 us  [near_exchange(): lax.all_to_all(value, 'coef', 0, 0, axis_index_groups=groups, tiled=True)]
  transfers between devices with their start and end apart: 2 -> 11, of which waited for: 2 -> 7; matrix products, arithmetic and copies ran while one was open for 1% -> 0% of each run, Pallas kernels for 0% -> 7%
where the time goes in v1:
time: 110 us; the launch traced here: 109 us
  starting transfers between devices  39.3 us (36%)
  blocking collectives  27.5 us (25%)
  waiting for transfers between devices  21.6 us (20%)
  Pallas kernels  17.4 us (16%)
  local copies, waits for them, and re-layouts  3.01 us (3%)
    all_to_all x1, blocking collectives, far_exchange(): lax.all_to_all(value, ('coef', 'band'), 0, 0, axis_index_groups=groups, t...  27.5 us
    ppermute x9, starting transfers between devices, along_band(): return lax.ppermute(value, 'band', band_perm(move))  26.7 us
    all_to_all x2, starting transfers between devices, near_exchange(): lax.all_to_all(value, 'coef', 0, 0, axis_index_groups=groups, tiled=True)  12.7 us
    all_to_all x2, waiting for transfers between devices, near_exchange(): lax.all_to_all(value, 'coef', 0, 0, axis_index_groups=groups, tiled=True)  12.2 us
    ppermute x9, waiting for transfers between devices, along_band(): return lax.ppermute(value, 'band', band_perm(move))  9.31 us
    pallas_call x1, Pallas kernels, finish(): pl.pallas_call(finish_kernel, in_specs=[smem] + [vmem] * 3 + [anywhere] *...  6.38 us
    pallas_call x1, Pallas kernels, intersect(): pl.pallas_call(intersect_kernel, in_specs=[smem] + [vmem] * (3 + N_SHARDS...  3.92 us
    pallas_call x1, Pallas kernels, stats(): pl.pallas_call(stats_kernel, in_specs=[anywhere, vmem], out_specs=[vmem,...  3.07 us
  transfers between devices with their start and end apart: 11, of which 7 were waited for; matrix products, arithmetic and copies ran while one was open for 0% of the time, Pallas kernels for 7%

profile of v1, /device:TPU:6, one launch (start us, length us, event | category | flops | bytes accessed | tf_op | source)
XLA Modules:
  0.0 109.0 jit_solution(982607125406629059)
XLA Ops:
  0.0 3.5 %collective-permute-start.2 = (bf16[32,4096]{1,0:T(8,128)(2,1)}, bf16[32,4096]{1,0:T(8,128)(2,1)S(1)}, u32[]{:S(2)}, u32[]{:S(2)}) collective-permute-start(bf16[32,4096]{1,0:T(8,128)(2,1)} %refs_0_.1), channel_id=1, source_target_pairs={{0,2},{1,7},{2,4},{3,1},{4,6},{5,3},{6,0},{7,5},{8,10},{9,15},{10,... | collective-permute-start | bytes 786440 | tf_op jit(solution)/shard_map/ppermute | solution.py:379
  3.5 3.6 %collective-permute-start.1 = (bf16[32,4096]{1,0:T(8,128)(2,1)}, bf16[32,4096]{1,0:T(8,128)(2,1)S(1)}, u32[]{:S(2)}, u32[]{:S(2)}) collective-permute-start(bf16[32,4096]{1,0:T(8,128)(2,1)} %refs_0_.1), channel_id=1, source_target_pairs={{0,6},{1,3},{2,0},{3,5},{4,2},{5,7},{6,4},{7,1},{8,14},{9,11},{10,... | collective-permute-start | bytes 786440 | tf_op jit(solution)/shard_map/ppermute | solution.py:379
  7.1 3.3 %collective-permute-start = (bf16[32,4096]{1,0:T(8,128)(2,1)}, bf16[32,4096]{1,0:T(8,128)(2,1)S(1)}, u32[]{:S(2)}, u32[]{:S(2)}) collective-permute-start(bf16[32,4096]{1,0:T(8,128)(2,1)} %refs_0_.1), channel_id=1, source_target_pairs={{0,8},{1,9},{2,10},{3,11},{4,12},{5,13},{6,14},{7,15},{8,0},{9,1},... | collective-permute-start | bytes 786440 | tf_op jit(solution)/shard_map/ppermute | solution.py:379
  10.4 0.0 collective-permute-done.2.refs_1_
  10.4 2.6 %collective-permute-start.3 = (bf16[32,4096]{1,0:T(8,128)(2,1)S(1)}, bf16[32,4096]{1,0:T(8,128)(2,1)S(1)}, u32[]{:S(2)}, u32[]{:S(2)}) collective-permute-start(bf16[32,4096]{1,0:T(8,128)(2,1)S(1)} %collective-permute-done.2.refs_1_), channel_id=1, source_target_pairs={{0,2},{1,7},{2,4},{3,1},{4,6},{5,3},{6,0},{7,5},{8,10},{9,15},{10,... | collective-permute-start | bytes 786440 | tf_op jit(solution)/shard_map/ppermute | solution.py:379
  13.0 0.0 copy-start
  13.0 0.8 copy-done
  13.9 0.0 copy-start.2
  13.9 3.1 %stats.1 = (f32[64,256]{1,0:T(8,128)S(1)}, bf16[256,4096]{1,0:T(8,128)(2,1)S(1)}) custom-call(bf16[256,4096]{1,0:T(8,128)(2,1)} %wave.1, s32[3,4096]{1,0:T(4,128)S(1)} %copy-done), custom_call_target="tpu_custom_call" | custom-call | flops 5242880 | bytes 2097152 | tf_op jit(solution)/shard_map/stats/pallas_call | solution.py:118
  16.9 0.0 collective-permute-done.1.refs_2_
  16.9 1.3 %collective-permute-done.refs_4_ = bf16[32,4096]{1,0:T(8,128)(2,1)S(1)} collective-permute-done((bf16[32,4096]{1,0:T(8,128)(2,1)}, bf16[32,4096]{1,0:T(8,128)(2,1)S(1)}, u32[]{:S(2)}, u32[]{:S(2)}) %collective-permute-start) | collective-permute-done | bytes 262176 | tf_op jit(solution)/shard_map/ppermute | solution.py:379
  18.2 1.6 %collective-permute-done.3.refs_3_ = bf16[32,4096]{1,0:T(8,128)(2,1)S(1)} collective-permute-done((bf16[32,4096]{1,0:T(8,128)(2,1)S(1)}, bf16[32,4096]{1,0:T(8,128)(2,1)S(1)}, u32[]{:S(2)}, u32[]{:S(2)}) %collective-permute-start.3) | collective-permute-done | bytes 262176 | tf_op jit(solution)/shard_map/ppermute | solution.py:379
  19.9 1.9 %collective-permute-start.4 = (bf16[256,4096]{1,0:T(8,128)(2,1)}, bf16[256,4096]{1,0:T(8,128)(2,1)}, u32[]{:S(2)}, u32[]{:S(2)}) collective-permute-start(bf16[256,4096]{1,0:T(8,128)(2,1)} %wave.1), channel_id=1, source_target_pairs={{0,1},{1,0},{2,3},{3,2},{4,5},{5,4},{6,7},{7,6},{8,9},{9,8},{10,11... | collective-permute-start | bytes 6291464 | tf_op jit(solution)/shard_map/ppermute | solution.py:379
  21.8 4.0 %collective-permute-start.7 = (bf16[32,4096]{1,0:T(8,128)(2,1)S(1)}, bf16[32,4096]{1,0:T(8,128)(2,1)}, u32[]{:S(2)}, u32[]{:S(2)}) collective-permute-start(bf16[32,4096]{1,0:T(8,128)(2,1)S(1)} %collective-permute-done.3.refs_3_), channel_id=1, source_target_pairs={{0,8},{1,9},{2,10},{3,11},{4,12},{5,13},{6,14},{7,15},{8,0},{9,1},... | collective-permute-start | bytes 786440 | tf_op jit(solution)/shard_map/ppermute | solution.py:379
  25.8 2.8 %collective-permute-start.6 = (bf16[32,4096]{1,0:T(8,128)(2,1)S(1)}, bf16[32,4096]{1,0:T(8,128)(2,1)}, u32[]{:S(2)}, u32[]{:S(2)}) collective-permute-start(bf16[32,4096]{1,0:T(8,128)(2,1)S(1)} %collective-permute-done.refs_4_), channel_id=1, source_target_pairs={{0,6},{1,3},{2,0},{3,5},{4,2},{5,7},{6,4},{7,1},{8,14},{9,11},{10,... | collective-permute-start | bytes 786440 | tf_op jit(solution)/shard_map/ppermute | solution.py:379
  28.6 3.1 %collective-permute-start.5 = (bf16[32,4096]{1,0:T(8,128)(2,1)S(1)}, bf16[32,4096]{1,0:T(8,128)(2,1)}, u32[]{:S(2)}, u32[]{:S(2)}) collective-permute-start(bf16[32,4096]{1,0:T(8,128)(2,1)S(1)} %collective-permute-done.refs_4_), channel_id=1, source_target_pairs={{0,2},{1,7},{2,4},{3,1},{4,6},{5,3},{6,0},{7,5},{8,10},{9,15},{10,... | collective-permute-start | bytes 786440 | tf_op jit(solution)/shard_map/ppermute | solution.py:379
  31.7 0.1 stack.43.place
  31.8 2.2 %collective-permute-done.7.refs_7_ = bf16[32,4096]{1,0:T(8,128)(2,1)} collective-permute-done((bf16[32,4096]{1,0:T(8,128)(2,1)S(1)}, bf16[32,4096]{1,0:T(8,128)(2,1)}, u32[]{:S(2)}, u32[]{:S(2)}) %collective-permute-start.7) | collective-permute-done | bytes 262176 | tf_op jit(solution)/shard_map/ppermute | solution.py:379
  34.0 1.8 %collective-permute-done.6.refs_6_ = bf16[32,4096]{1,0:T(8,128)(2,1)} collective-permute-done((bf16[32,4096]{1,0:T(8,128)(2,1)S(1)}, bf16[32,4096]{1,0:T(8,128)(2,1)}, u32[]{:S(2)}, u32[]{:S(2)}) %collective-permute-start.6) | collective-permute-done | bytes 262176 | tf_op jit(solution)/shard_map/ppermute | solution.py:379
  35.8 2.4 %collective-permute-done.5.refs_5_ = bf16[32,4096]{1,0:T(8,128)(2,1)} collective-permute-done((bf16[32,4096]{1,0:T(8,128)(2,1)S(1)}, bf16[32,4096]{1,0:T(8,128)(2,1)}, u32[]{:S(2)}, u32[]{:S(2)}) %collective-permute-start.5) | collective-permute-done | bytes 262176 | tf_op jit(solution)/shard_map/ppermute | solution.py:379
  38.2 0.0 collective-permute-done.4.wave_other
  38.2 0.0 copy-done.2
  38.2 0.0 copy-start.5
  38.2 3.9 %intersect.1 = (bf16[576,256]{1,0:T(8,128)(2,1)}, bf16[256,4096]{1,0:T(8,128)(2,1)}) custom-call(s32[10]{0:T(128)S(1)} %stack.43.place, f32[64,256]{1,0:T(8,128)S(1)} %get-tuple-element.21.stat, bf16[256,4096]{1,0:T(8,128)(2,1)S(1)} %get-tuple-element.22.wave_own.wave, bf16[256,4096]{1,0:T(8,128)(2,1)} %collective-permute-done.4.wave_other, ...), custom_call_target="tpu_custom_call" | custom-call | flops 1073741824 | bytes 8388608 | tf_op jit(solution)/shard_map/intersect/pallas_call | solution.py:187
  42.1 7.4 %all-to-all-start = ((bf16[8,72,256]{2,1,0:T(8,128)(2,1)}), bf16[8,72,256]{2,1,0:T(8,128)(2,1)S(1)}, u32[]{:S(2)}, u32[]{:S(2)}) async-start(bf16[8,72,256]{2,1,0:T(8,128)(2,1)} %bitcast.10), calls=%async_computation | async-start | bytes 589824 | tf_op jit(solution)/shard_map/all_to_all | solution.py:400
  49.6 1.9 %collective-permute-start.8 = (bf16[256,4096]{1,0:T(8,128)(2,1)}, bf16[256,4096]{1,0:T(8,128)(2,1)}, u32[]{:S(2)}, u32[]{:S(2)}) collective-permute-start(bf16[256,4096]{1,0:T(8,128)(2,1)} %get-tuple-element.34.whole_own), channel_id=1, source_target_pairs={{0,1},{1,0},{2,3},{3,2},{4,5},{5,4},{6,7},{7,6},{8,9},{9,8},{10,11... | collective-permute-start | bytes 6291464 | tf_op jit(solution)/shard_map/ppermute | solution.py:379
  51.5 0.0 copy-done.5
  51.5 0.0 copy-start.3
  51.5 1.0 copy-done.3
  52.5 0.0 copy-start.4
  52.5 1.0 copy-done.4
  53.6 1.5 %masked_weights.1.weights = bf16[512,1024]{1,0:T(8,128)(2,1)S(1)} custom-call(s32[1,512]{1,0:T(1,128)S(1)} %bitcast.21, bf16[512,512]{1,0:T(8,128)(2,1)S(1)} %copy-done.3, bf16[512,512]{1,0:T(8,128)(2,1)S(1)} %copy-done.4), custom_call_target="tpu_custom_call" | custom-call | flops 1207959552 | bytes 2097152 | tf_op jit(solution)/shard_map/masked_weights/pallas_call | solution.py:148
  55.1 0.0 copy-start.1
  55.1 3.6 %all-to-all-done = bf16[8,72,256]{2,1,0:T(8,128)(2,1)S(1)} async-done(((bf16[8,72,256]{2,1,0:T(8,128)(2,1)}), bf16[8,72,256]{2,1,0:T(8,128)(2,1)S(1)}, u32[]{:S(2)}, u32[]{:S(2)}) %all-to-all-start) | async-done | bytes 294944 | tf_op jit(solution)/shard_map/all_to_all | solution.py:400
  58.7 0.7 near_sum.1
  59.4 27.5 %all_to_all.34 = bf16[8,40,256]{2,1,0:T(8,128)(2,1)S(1)} all-to-all(bf16[8,40,256]{2,1,0:T(8,128)(2,1)S(1)} %bitcast.20), channel_id=1, replica_groups={{0,1,128,129,256,257,384,385},{2,3,130,131,258,259,386,387},{4,5,132,13..., dimensions={0} | all-to-all | bytes 327680 | tf_op jit(solution)/shard_map/all_to_all | solution.py:408
  86.9 1.8 %couple.1 = bf16[576,256]{1,0:T(8,128)(2,1)} custom-call(s32[10]{0:T(128)S(1)} %stack.43.place, f32[32,256]{1,0:T(8,128)S(1)} %get-tuple-element.31.keep, bf16[320,256]{1,0:T(8,128)(2,1)S(1)} %bitcast.19, bf16[512,1024]{1,0:T(8,128)(2,1)S(1)} %masked_weights.1.weights), custom_call_target="tpu_custom_call" | custom-call | flops 100663296 | bytes 1572864 | tf_op jit(solution)/shard_map/couple/pallas_call | solution.py:264
  88.7 5.2 %all-to-all-start.2 = ((bf16[8,72,256]{2,1,0:T(8,128)(2,1)}), bf16[8,72,256]{2,1,0:T(8,128)(2,1)S(1)}, u32[]{:S(2)}, u32[]{:S(2)}) async-start(bf16[8,72,256]{2,1,0:T(8,128)(2,1)} %bitcast.15), calls=%async_computation.2 | async-start | bytes 589824 | tf_op jit(solution)/shard_map/all_to_all | solution.py:400
  94.0 0.0 collective-permute-done.8.whole_other
  94.0 8.7 %all-to-all-done.2 = bf16[8,72,256]{2,1,0:T(8,128)(2,1)S(1)} async-done(((bf16[8,72,256]{2,1,0:T(8,128)(2,1)}), bf16[8,72,256]{2,1,0:T(8,128)(2,1)S(1)}, u32[]{:S(2)}, u32[]{:S(2)}) %all-to-all-start.2) | async-done | bytes 294944 | tf_op jit(solution)/shard_map/all_to_all | solution.py:400
  102.6 0.0 copy-done.1
  102.6 6.4 %finish.1 = bf16[256,4096]{1,0:T(8,128)(2,1)} custom-call(s32[10]{0:T(128)S(1)} %stack.43.place, bf16[576,256]{1,0:T(8,128)(2,1)S(1)} %bitcast.17, s32[3,4096]{1,0:T(4,128)S(1)} %copy-done.1, bf16[256,4096]{1,0:T(8,128)(2,1)S(1)} %get-tuple-element.22.wave_own.wave, bf16[256,4096]{1,0:T(8,128)(2,1)} %get-tuple-element.34.whole_own, ...), custom_call_target="tpu_custom_call" | custom-call | flops 1073741824 | bytes 8388608 | tf_op jit(solution)/shard_map/finish/pallas_call | solution.py:355
Async XLA Ops:
  0.0 10.4 %collective-permute-start.2 = (bf16[32,4096]{1,0:T(8,128)(2,1)}, bf16[32,4096]{1,0:T(8,128)(2,1)S(1)}, u32[]{:S(2)}, u32[]{:S(2)}) collective-permute-start(bf16[32,4096]{1,0:T(8,128)(2,1)} %refs_0_.1), channel_id=1, source_target_pairs={{0,2},{1,7},{2,4},{3,1},{4,6},{5,3},{6,0},{7,5},{8,10},{9,15},{10,... | collective-permute-start | bytes 786440 | tf_op jit(solution)/shard_map/ppermute | solution.py:379
  3.5 13.5 %collective-permute-start.1 = (bf16[32,4096]{1,0:T(8,128)(2,1)}, bf16[32,4096]{1,0:T(8,128)(2,1)S(1)}, u32[]{:S(2)}, u32[]{:S(2)}) collective-permute-start(bf16[32,4096]{1,0:T(8,128)(2,1)} %refs_0_.1), channel_id=1, source_target_pairs={{0,6},{1,3},{2,0},{3,5},{4,2},{5,7},{6,4},{7,1},{8,14},{9,11},{10,... | collective-permute-start | bytes 786440 | tf_op jit(solution)/shard_map/ppermute | solution.py:379
  7.1 11.2 %collective-permute-start = (bf16[32,4096]{1,0:T(8,128)(2,1)}, bf16[32,4096]{1,0:T(8,128)(2,1)S(1)}, u32[]{:S(2)}, u32[]{:S(2)}) collective-permute-start(bf16[32,4096]{1,0:T(8,128)(2,1)} %refs_0_.1), channel_id=1, source_target_pairs={{0,8},{1,9},{2,10},{3,11},{4,12},{5,13},{6,14},{7,15},{8,0},{9,1},... | collective-permute-start | bytes 786440 | tf_op jit(solution)/shard_map/ppermute | solution.py:379
  10.4 9.5 %collective-permute-start.3 = (bf16[32,4096]{1,0:T(8,128)(2,1)S(1)}, bf16[32,4096]{1,0:T(8,128)(2,1)S(1)}, u32[]{:S(2)}, u32[]{:S(2)}) collective-permute-start(bf16[32,4096]{1,0:T(8,128)(2,1)S(1)} %collective-permute-done.2.refs_1_), channel_id=1, source_target_pairs={{0,2},{1,7},{2,4},{3,1},{4,6},{5,3},{6,0},{7,5},{8,10},{9,15},{10,... | collective-permute-start | bytes 786440 | tf_op jit(solution)/shard_map/ppermute | solution.py:379
  13.0 0.8 copy-start
  13.9 24.3 %copy-start.2 = (bf16[32,4096]{1,0:T(8,128)(2,1)S(1)}, bf16[32,4096]{1,0:T(8,128)(2,1)}, u32[]{:S(2)}) copy-start(bf16[32,4096]{1,0:T(8,128)(2,1)} %refs_0_.1) | copy-start | bytes 786436
  19.9 18.3 %collective-permute-start.4 = (bf16[256,4096]{1,0:T(8,128)(2,1)}, bf16[256,4096]{1,0:T(8,128)(2,1)}, u32[]{:S(2)}, u32[]{:S(2)}) collective-permute-start(bf16[256,4096]{1,0:T(8,128)(2,1)} %wave.1), channel_id=1, source_target_pairs={{0,1},{1,0},{2,3},{3,2},{4,5},{5,4},{6,7},{7,6},{8,9},{9,8},{10,11... | collective-permute-start | bytes 6291464 | tf_op jit(solution)/shard_map/ppermute | solution.py:379
  21.8 12.2 %collective-permute-start.7 = (bf16[32,4096]{1,0:T(8,128)(2,1)S(1)}, bf16[32,4096]{1,0:T(8,128)(2,1)}, u32[]{:S(2)}, u32[]{:S(2)}) collective-permute-start(bf16[32,4096]{1,0:T(8,128)(2,1)S(1)} %collective-permute-done.3.refs_3_), channel_id=1, source_target_pairs={{0,8},{1,9},{2,10},{3,11},{4,12},{5,13},{6,14},{7,15},{8,0},{9,1},... | collective-permute-start | bytes 786440 | tf_op jit(solution)/shard_map/ppermute | solution.py:379
  25.8 10.0 %collective-permute-start.6 = (bf16[32,4096]{1,0:T(8,128)(2,1)S(1)}, bf16[32,4096]{1,0:T(8,128)(2,1)}, u32[]{:S(2)}, u32[]{:S(2)}) collective-permute-start(bf16[32,4096]{1,0:T(8,128)(2,1)S(1)} %collective-permute-done.refs_4_), channel_id=1, source_target_pairs={{0,6},{1,3},{2,0},{3,5},{4,2},{5,7},{6,4},{7,1},{8,14},{9,11},{10,... | collective-permute-start | bytes 786440 | tf_op jit(solution)/shard_map/ppermute | solution.py:379
  28.6 9.6 %collective-permute-start.5 = (bf16[32,4096]{1,0:T(8,128)(2,1)S(1)}, bf16[32,4096]{1,0:T(8,128)(2,1)}, u32[]{:S(2)}, u32[]{:S(2)}) collective-permute-start(bf16[32,4096]{1,0:T(8,128)(2,1)S(1)} %collective-permute-done.refs_4_), channel_id=1, source_target_pairs={{0,2},{1,7},{2,4},{3,1},{4,6},{5,3},{6,0},{7,5},{8,10},{9,15},{10,... | collective-permute-start | bytes 786440 | tf_op jit(solution)/shard_map/ppermute | solution.py:379
  38.2 13.3 %copy-start.5 = (s32[512]{0:T(512)S(1)}, s32[512]{0:T(512)}, u32[]{:S(2)}) copy-start(s32[512]{0:T(512)} %param.9) | copy-start | bytes 6148
  42.1 16.6 %all-to-all-start = ((bf16[8,72,256]{2,1,0:T(8,128)(2,1)}), bf16[8,72,256]{2,1,0:T(8,128)(2,1)S(1)}, u32[]{:S(2)}, u32[]{:S(2)}) async-start(bf16[8,72,256]{2,1,0:T(8,128)(2,1)} %bitcast.10), calls=%async_computation | async-start | bytes 589824 | tf_op jit(solution)/shard_map/all_to_all | solution.py:400
  49.6 44.4 %collective-permute-start.8 = (bf16[256,4096]{1,0:T(8,128)(2,1)}, bf16[256,4096]{1,0:T(8,128)(2,1)}, u32[]{:S(2)}, u32[]{:S(2)}) collective-permute-start(bf16[256,4096]{1,0:T(8,128)(2,1)} %get-tuple-element.34.whole_own), channel_id=1, source_target_pairs={{0,1},{1,0},{2,3},{3,2},{4,5},{5,4},{6,7},{7,6},{8,9},{9,8},{10,11... | collective-permute-start | bytes 6291464 | tf_op jit(solution)/shard_map/ppermute | solution.py:379
  51.5 1.0 copy-start.3
  52.5 1.0 copy-start.4
  55.1 47.5 %copy-start.1 = (s32[3,4096]{1,0:T(4,128)S(1)}, s32[3,4096]{1,0:T(4,128)}, u32[]{:S(2)}) copy-start(s32[3,4096]{1,0:T(4,128)} %gvec.3) | copy-start | bytes 147460
  88.7 13.9 %all-to-all-start.2 = ((bf16[8,72,256]{2,1,0:T(8,128)(2,1)}), bf16[8,72,256]{2,1,0:T(8,128)(2,1)S(1)}, u32[]{:S(2)}, u32[]{:S(2)}) async-start(bf16[8,72,256]{2,1,0:T(8,128)(2,1)} %bitcast.15), calls=%async_computation.2 | async-start | bytes 589824 | tf_op jit(solution)/shard_map/all_to_all | solution.py:400

commit v2 on v1

--- a/solution.py
+++ b/solution.py
@@ -153,7 +153,7 @@
         compiler_params=params(24),
         cost_estimate=cost(9 * NPROJ ** 3, 8 * NPROJ * NPROJ),
         name="masked_weights",
-    )(atom_of.reshape(1, NPROJ), dion, qaug)
+    )(atom_of.reshape(1, NPROJ), in_hbm(dion), in_hbm(qaug))
 
 
 def against(left, right):
@@ -272,21 +272,22 @@
     )(place, keep, received, weights)
 
 
-TILE = 256
+TILE = 512
 N_TILES = COLS // TILE
 CHUNK = 16
 
 
 def finish_kernel(place, coupled, gvec, wave, whole_own, whole_other, out,
-                  own_v, other_v, out_v, halves_v, energy_v, scale_v, even_v, odd_v, sems, out_sems):
+                  whole_v, out_v, halves_v, energy_v, scale_v, even_v, odd_v, sems, out_sems):
     def columns(tile):
         return pl.ds(pl.multiple_of(tile * TILE, TILE), TILE)
 
     def copies(tile):
         cols = columns(tile)
         return [
-            pltpu.make_async_copy(whole_own.at[:, cols], own_v.at[:, cols], sems.at[tile, 0]),
-            pltpu.make_async_copy(whole_other.at[:, cols], other_v.at[:, cols], sems.at[tile, 1]),
+            pltpu.make_async_copy(
+                source.at[:, cols], whole_v.at[pl.ds(i * HALF_PROJ, HALF_PROJ), cols], sems.at[tile, i])
+            for i, source in enumerate((whole_own, whole_other))
         ]
 
     def out_copy(tile):
@@ -299,8 +300,7 @@
 
     def expand(tile, expanded_v):
         cols = columns(tile)
-        expanded_v[...] = jnp.dot(halves_v[:ROWS, :], own_v[:, cols], preferred_element_type=f32) + jnp.dot(
-            halves_v[ROWS:, :], other_v[:, cols], preferred_element_type=f32)
+        expanded_v[...] = jnp.dot(halves_v[...], whole_v[:, cols], preferred_element_type=f32)
 
     def conclude(tile, expanded_v):
         cols = columns(tile)
@@ -324,8 +324,8 @@
     for n in range(NEAR):
         rows = slice(n * BANDS, (n + 1) * BANDS)
         first, second = blocks[n, :BANDS].astype(bf16), blocks[n, BANDS:2 * BANDS].astype(bf16)
-        halves_v[rows, :] = jnp.where(core == 0, first, second)
-        halves_v[ROWS + n * BANDS:ROWS + (n + 1) * BANDS, :] = jnp.where(core == 0, second, first)
+        halves_v[rows, :HALF_PROJ] = jnp.where(core == 0, first, second)
+        halves_v[rows, HALF_PROJ:] = jnp.where(core == 0, second, first)
         energy, ekin = from_rows(blocks[n, 2 * BANDS:])
         energy_v[rows, :] = jnp.broadcast_to(energy, (BANDS, 128))
         scale_v[rows, :] = jnp.broadcast_to((2.0 / 3.0) / ekin, (BANDS, 128))
@@ -357,8 +357,7 @@
         in_specs=[smem] + [vmem] * 3 + [anywhere] * 2,
         out_specs=anywhere,
         out_shape=jax.ShapeDtypeStruct((ROWS, COLS), bf16),
-        scratch_shapes=[pltpu.VMEM((HALF_PROJ, COLS), bf16)] * 2
-        + [pltpu.VMEM((ROWS, COLS), bf16), pltpu.VMEM((2 * ROWS, HALF_PROJ), bf16)]
+        scratch_shapes=[pltpu.VMEM((NPROJ, COLS), bf16), pltpu.VMEM((ROWS, COLS), bf16), pltpu.VMEM((ROWS, NPROJ), bf16)]
         + [pltpu.VMEM((ROWS, 128), f32)] * 2 + [pltpu.VMEM((ROWS, TILE), f32)] * 2
         + [pltpu.SemaphoreType.DMA((N_TILES, 2)), pltpu.SemaphoreType.DMA((N_TILES,))],
         compiler_params=params(24),
@@ -419,17 +418,16 @@
     before, after = ring(projector), against_ring(projector)
     far = ring(before)
     stat, wave_v = stats(wave, gvec)
-    across, after, far, own_wave, stat = lax.optimization_barrier((across, after, far, wave, stat))
+    across, after, far, own_wave, stat, late_dion = lax.optimization_barrier((across, after, far, wave, stat, dion))
     far_x = to_other_x(far)
     before_x, after_x = ring(across), against_ring(across)
     wave_other = swap(own_wave)
     shards = [projector, before, after, far, across, before_x, after_x, far_x]
+    weights = masked_weights(atom_of, late_dion, qaug)
+    stat, weights = lax.optimization_barrier((stat, weights))
     message, whole = intersect(place, stat, wave_v, wave_other, shards)
-    message, dion = lax.optimization_barrier((message, dion))
-    weights = masked_weights(atom_of, dion, qaug)
-
-    received, weights = lax.optimization_barrier((near_exchange(message), weights))
-    keep, message = near_sum(place, received)
+
+    keep, message = near_sum(place, near_exchange(message))
     coupled = near_exchange(couple(place, keep, far_exchange(message), weights))
     return finish(place, coupled, wave_v, gvec, whole, swap(whole))
 

time: 110 us -> 110 us (level)
    all_to_all x2, waiting for transfers between devices: 12.2 us -> 15.9 us  [near_exchange(): lax.all_to_all(value, 'coef', 0, 0, axis_index_groups=groups, tiled=True)]
    ppermute x9, waiting for transfers between devices: 9.31 us -> 6.16 us  [along_band(): return lax.ppermute(value, 'band', band_perm(move))]
    pallas_call x1, Pallas kernels: 1.52 us -> 2.76 us  [masked_weights(): pl.pallas_call(weights_kernel, in_specs=[vmem] * 3, out_specs=vmem, out_s...]
    unnamed x12 -> x14, local copies, waits for them, and re-layouts: 2.93 us -> 2.26 us
  transfers between devices with their start and end apart: 11 -> 11, of which waited for: 7 -> 6; matrix products, arithmetic and copies ran while one was open for 0% -> 0% of each run, Pallas kernels for 7% -> 8%
where the time goes in v2:
time: 110 us; the launch traced here: 109 us
  starting transfers between devices  39.5 us (36%)
  blocking collectives  27.3 us (25%)
  waiting for transfers between devices  22 us (20%)
  Pallas kernels  17.6 us (16%)
  local copies, waits for them, and re-layouts  2.35 us (2%)
    all_to_all x1, blocking collectives, far_exchange(): lax.all_to_all(value, ('coef', 'band'), 0, 0, axis_index_groups=groups, t...  27.3 us
    ppermute x9, starting transfers between devices, along_band(): return lax.ppermute(value, 'band', band_perm(move))  26.7 us
    all_to_all x2, waiting for transfers between devices, near_exchange(): lax.all_to_all(value, 'coef', 0, 0, axis_index_groups=groups, tiled=True)  15.9 us
    all_to_all x2, starting transfers between devices, near_exchange(): lax.all_to_all(value, 'coef', 0, 0, axis_index_groups=groups, tiled=True)  12.9 us
    ppermute x9, waiting for transfers between devices, along_band(): return lax.ppermute(value, 'band', band_perm(move))  6.16 us
    pallas_call x1, Pallas kernels, finish(): pl.pallas_call(finish_kernel, in_specs=[smem] + [vmem] * 3 + [anywhere] *...  5.93 us
    pallas_call x1, Pallas kernels, intersect(): pl.pallas_call(intersect_kernel, in_specs=[smem] + [vmem] * (3 + N_SHARDS...  3.36 us
    pallas_call x1, Pallas kernels, stats(): pl.pallas_call(stats_kernel, in_specs=[anywhere, vmem], out_specs=[vmem,...  3.04 us
  transfers between devices with their start and end apart: 11, of which 6 were waited for; matrix products, arithmetic and copies ran while one was open for 0% of the time, Pallas kernels for 8%

profile of v2, /device:TPU:6, one launch (start us, length us, event | category | flops | bytes accessed | tf_op | source)
XLA Modules:
  0.0 109.1 jit_solution(12975304052576563435)
XLA Ops:
  0.0 3.5 %collective-permute-start.2 = (bf16[32,4096]{1,0:T(8,128)(2,1)}, bf16[32,4096]{1,0:T(8,128)(2,1)S(1)}, u32[]{:S(2)}, u32[]{:S(2)}) collective-permute-start(bf16[32,4096]{1,0:T(8,128)(2,1)} %refs_0_.1), channel_id=1, source_target_pairs={{0,2},{1,7},{2,4},{3,1},{4,6},{5,3},{6,0},{7,5},{8,10},{9,15},{10,... | collective-permute-start | bytes 786440 | tf_op jit(solution)/shard_map/ppermute | solution.py:378
  3.5 3.6 %collective-permute-start.1 = (bf16[32,4096]{1,0:T(8,128)(2,1)}, bf16[32,4096]{1,0:T(8,128)(2,1)S(1)}, u32[]{:S(2)}, u32[]{:S(2)}) collective-permute-start(bf16[32,4096]{1,0:T(8,128)(2,1)} %refs_0_.1), channel_id=1, source_target_pairs={{0,6},{1,3},{2,0},{3,5},{4,2},{5,7},{6,4},{7,1},{8,14},{9,11},{10,... | collective-permute-start | bytes 786440 | tf_op jit(solution)/shard_map/ppermute | solution.py:378
  7.1 3.3 %collective-permute-start = (bf16[32,4096]{1,0:T(8,128)(2,1)}, bf16[32,4096]{1,0:T(8,128)(2,1)}, u32[]{:S(2)}, u32[]{:S(2)}) collective-permute-start(bf16[32,4096]{1,0:T(8,128)(2,1)} %refs_0_.1), channel_id=1, source_target_pairs={{0,8},{1,9},{2,10},{3,11},{4,12},{5,13},{6,14},{7,15},{8,0},{9,1},... | collective-permute-start | bytes 786440 | tf_op jit(solution)/shard_map/ppermute | solution.py:378
  10.4 0.0 collective-permute-done.2.refs_1_
  10.4 2.6 %collective-permute-start.3 = (bf16[32,4096]{1,0:T(8,128)(2,1)S(1)}, bf16[32,4096]{1,0:T(8,128)(2,1)}, u32[]{:S(2)}, u32[]{:S(2)}) collective-permute-start(bf16[32,4096]{1,0:T(8,128)(2,1)S(1)} %collective-permute-done.2.refs_1_), channel_id=1, source_target_pairs={{0,2},{1,7},{2,4},{3,1},{4,6},{5,3},{6,0},{7,5},{8,10},{9,15},{10,... | collective-permute-start | bytes 786440 | tf_op jit(solution)/shard_map/ppermute | solution.py:378
  13.0 0.0 copy-start.1
  13.0 0.8 copy-done.1
  13.9 0.0 copy-start.6
  13.9 3.0 %stats.1 = (f32[64,256]{1,0:T(8,128)S(1)}, bf16[256,4096]{1,0:T(8,128)(2,1)S(1)}) custom-call(bf16[256,4096]{1,0:T(8,128)(2,1)} %wave.1, s32[3,4096]{1,0:T(4,128)S(1)} %copy-done.1), custom_call_target="tpu_custom_call" | custom-call | flops 5242880 | bytes 2097152 | tf_op jit(solution)/shard_map/stats/pallas_call | solution.py:118
  16.9 0.0 collective-permute-done.1.refs_2_
  16.9 0.0 copy-start.4
  16.9 0.7 copy-done.4
  17.6 0.7 collective-permute-done.refs_4_
  18.3 1.6 %collective-permute-done.3.refs_3_ = bf16[32,4096]{1,0:T(8,128)(2,1)} collective-permute-done((bf16[32,4096]{1,0:T(8,128)(2,1)S(1)}, bf16[32,4096]{1,0:T(8,128)(2,1)}, u32[]{:S(2)}, u32[]{:S(2)}) %collective-permute-start.3) | collective-permute-done | bytes 262176 | tf_op jit(solution)/shard_map/ppermute | solution.py:378
  20.0 1.9 %collective-permute-start.4 = (bf16[256,4096]{1,0:T(8,128)(2,1)}, bf16[256,4096]{1,0:T(8,128)(2,1)}, u32[]{:S(2)}, u32[]{:S(2)}) collective-permute-start(bf16[256,4096]{1,0:T(8,128)(2,1)} %wave.1), channel_id=1, source_target_pairs={{0,1},{1,0},{2,3},{3,2},{4,5},{5,4},{6,7},{7,6},{8,9},{9,8},{10,11... | collective-permute-start | bytes 6291464 | tf_op jit(solution)/shard_map/ppermute | solution.py:378
  21.9 4.0 %collective-permute-start.7 = (bf16[32,4096]{1,0:T(8,128)(2,1)}, bf16[32,4096]{1,0:T(8,128)(2,1)}, u32[]{:S(2)}, u32[]{:S(2)}) collective-permute-start(bf16[32,4096]{1,0:T(8,128)(2,1)} %collective-permute-done.3.refs_3_), channel_id=1, source_target_pairs={{0,8},{1,9},{2,10},{3,11},{4,12},{5,13},{6,14},{7,15},{8,0},{9,1},... | collective-permute-start | bytes 786440 | tf_op jit(solution)/shard_map/ppermute | solution.py:378
  25.9 2.8 %collective-permute-start.6 = (bf16[32,4096]{1,0:T(8,128)(2,1)}, bf16[32,4096]{1,0:T(8,128)(2,1)}, u32[]{:S(2)}, u32[]{:S(2)}) collective-permute-start(bf16[32,4096]{1,0:T(8,128)(2,1)} %collective-permute-done.refs_4_), channel_id=1, source_target_pairs={{0,6},{1,3},{2,0},{3,5},{4,2},{5,7},{6,4},{7,1},{8,14},{9,11},{10,... | collective-permute-start | bytes 786440 | tf_op jit(solution)/shard_map/ppermute | solution.py:378
  28.7 3.1 %collective-permute-start.5 = (bf16[32,4096]{1,0:T(8,128)(2,1)}, bf16[32,4096]{1,0:T(8,128)(2,1)}, u32[]{:S(2)}, u32[]{:S(2)}) collective-permute-start(bf16[32,4096]{1,0:T(8,128)(2,1)} %collective-permute-done.refs_4_), channel_id=1, source_target_pairs={{0,2},{1,7},{2,4},{3,1},{4,6},{5,3},{6,0},{7,5},{8,10},{9,15},{10,... | collective-permute-start | bytes 786440 | tf_op jit(solution)/shard_map/ppermute | solution.py:378
  31.8 0.1 stack.43.place
  31.9 0.0 copy-done.6
  31.9 0.0 copy-start.3
  31.9 0.0 copy-start.5
  31.9 2.8 %masked_weights.1.weights = bf16[512,1024]{1,0:T(8,128)(2,1)S(1)} custom-call(s32[1,512]{1,0:T(1,128)S(1)} %bitcast.22, bf16[512,512]{1,0:T(8,128)(2,1)} %dion, bf16[512,512]{1,0:T(8,128)(2,1)} %qaug.1), custom_call_target="tpu_custom_call" | custom-call | flops 1207959552 | bytes 2097152 | tf_op jit(solution)/shard_map/masked_weights/pallas_call | solution.py:148
  34.7 0.0 collective-permute-done.7.refs_7_
  34.7 1.4 %collective-permute-done.6.refs_6_ = bf16[32,4096]{1,0:T(8,128)(2,1)} collective-permute-done((bf16[32,4096]{1,0:T(8,128)(2,1)}, bf16[32,4096]{1,0:T(8,128)(2,1)}, u32[]{:S(2)}, u32[]{:S(2)}) %collective-permute-start.6) | collective-permute-done | bytes 262176 | tf_op jit(solution)/shard_map/ppermute | solution.py:378
  36.1 2.4 %collective-permute-done.5.refs_5_ = bf16[32,4096]{1,0:T(8,128)(2,1)} collective-permute-done((bf16[32,4096]{1,0:T(8,128)(2,1)}, bf16[32,4096]{1,0:T(8,128)(2,1)}, u32[]{:S(2)}, u32[]{:S(2)}) %collective-permute-start.5) | collective-permute-done | bytes 262176 | tf_op jit(solution)/shard_map/ppermute | solution.py:378
  38.5 0.0 collective-permute-done.4.wave_other
  38.5 0.0 copy-done.3
  38.5 0.0 copy-done.5
  38.5 3.4 %intersect.1 = (bf16[576,256]{1,0:T(8,128)(2,1)S(1)}, bf16[256,4096]{1,0:T(8,128)(2,1)}) custom-call(s32[10]{0:T(128)S(1)} %stack.43.place, f32[64,256]{1,0:T(8,128)S(1)} %get-tuple-element.22.stat, bf16[256,4096]{1,0:T(8,128)(2,1)S(1)} %get-tuple-element.23.wave_own.wave, bf16[256,4096]{1,0:T(8,128)(2,1)} %collective-permute-done.4.wave_other, ...), custom_call_target="tpu_custom_call" | custom-call | flops 1073741824 | bytes 8388608 | tf_op jit(solution)/shard_map/intersect/pallas_call | solution.py:187
  41.9 0.0 copy-start
  41.9 0.7 copy-done
  42.6 0.0 copy-start.2
  42.6 7.6 %all-to-all-start = ((bf16[8,72,256]{2,1,0:T(8,128)(2,1)}), bf16[8,72,256]{2,1,0:T(8,128)(2,1)S(1)}, u32[]{:S(2)}, u32[]{:S(2)}) async-start(bf16[8,72,256]{2,1,0:T(8,128)(2,1)} %bitcast.20), calls=%async_computation | async-start | bytes 589824 | tf_op jit(solution)/shard_map/all_to_all | solution.py:399
  50.2 1.9 %collective-permute-start.8 = (bf16[256,4096]{1,0:T(8,128)(2,1)}, bf16[256,4096]{1,0:T(8,128)(2,1)}, u32[]{:S(2)}, u32[]{:S(2)}) collective-permute-start(bf16[256,4096]{1,0:T(8,128)(2,1)} %get-tuple-element.32.whole_own), channel_id=1, source_target_pairs={{0,1},{1,0},{2,3},{3,2},{4,5},{5,4},{6,7},{7,6},{8,9},{9,8},{10,11... | collective-permute-start | bytes 6291464 | tf_op jit(solution)/shard_map/ppermute | solution.py:378
  52.1 7.2 %all-to-all-done = bf16[8,72,256]{2,1,0:T(8,128)(2,1)S(1)} async-done(((bf16[8,72,256]{2,1,0:T(8,128)(2,1)}), bf16[8,72,256]{2,1,0:T(8,128)(2,1)S(1)}, u32[]{:S(2)}, u32[]{:S(2)}) %all-to-all-start) | async-done | bytes 294944 | tf_op jit(solution)/shard_map/all_to_all | solution.py:399
  59.3 0.7 near_sum.1
  60.0 27.3 %all_to_all.33 = bf16[8,40,256]{2,1,0:T(8,128)(2,1)S(1)} all-to-all(bf16[8,40,256]{2,1,0:T(8,128)(2,1)S(1)} %bitcast.21), channel_id=1, replica_groups={{0,1,128,129,256,257,384,385},{2,3,130,131,258,259,386,387},{4,5,132,13..., dimensions={0} | all-to-all | bytes 327680 | tf_op jit(solution)/shard_map/all_to_all | solution.py:407
  87.4 1.8 %couple.1 = bf16[576,256]{1,0:T(8,128)(2,1)} custom-call(s32[10]{0:T(128)S(1)} %stack.43.place, f32[32,256]{1,0:T(8,128)S(1)} %get-tuple-element.29.keep, bf16[320,256]{1,0:T(8,128)(2,1)S(1)} %bitcast.19, bf16[512,1024]{1,0:T(8,128)(2,1)S(1)} %masked_weights.1.weights), custom_call_target="tpu_custom_call" | custom-call | flops 100663296 | bytes 1572864 | tf_op jit(solution)/shard_map/couple/pallas_call | solution.py:264
  89.2 5.3 %all-to-all-start.2 = ((bf16[8,72,256]{2,1,0:T(8,128)(2,1)}), bf16[8,72,256]{2,1,0:T(8,128)(2,1)S(1)}, u32[]{:S(2)}, u32[]{:S(2)}) async-start(bf16[8,72,256]{2,1,0:T(8,128)(2,1)} %bitcast.15), calls=%async_computation.2 | async-start | bytes 589824 | tf_op jit(solution)/shard_map/all_to_all | solution.py:399
  94.5 0.0 collective-permute-done.8.whole_other
  94.5 8.7 %all-to-all-done.2 = bf16[8,72,256]{2,1,0:T(8,128)(2,1)S(1)} async-done(((bf16[8,72,256]{2,1,0:T(8,128)(2,1)}), bf16[8,72,256]{2,1,0:T(8,128)(2,1)S(1)}, u32[]{:S(2)}, u32[]{:S(2)}) %all-to-all-start.2) | async-done | bytes 294944 | tf_op jit(solution)/shard_map/all_to_all | solution.py:399
  103.1 0.0 copy-done.2
  103.1 5.9 %finish.1 = bf16[256,4096]{1,0:T(8,128)(2,1)} custom-call(s32[10]{0:T(128)S(1)} %stack.43.place, bf16[576,256]{1,0:T(8,128)(2,1)S(1)} %bitcast.17, s32[3,4096]{1,0:T(4,128)S(1)} %copy-done.2, bf16[256,4096]{1,0:T(8,128)(2,1)S(1)} %get-tuple-element.23.wave_own.wave, bf16[256,4096]{1,0:T(8,128)(2,1)} %get-tuple-element.32.whole_own, ...), custom_call_target="tpu_custom_call" | custom-call | flops 1073741824 | bytes 8388608 | tf_op jit(solution)/shard_map/finish/pallas_call | solution.py:355
Async XLA Ops:
  0.0 10.4 %collective-permute-start.2 = (bf16[32,4096]{1,0:T(8,128)(2,1)}, bf16[32,4096]{1,0:T(8,128)(2,1)S(1)}, u32[]{:S(2)}, u32[]{:S(2)}) collective-permute-start(bf16[32,4096]{1,0:T(8,128)(2,1)} %refs_0_.1), channel_id=1, source_target_pairs={{0,2},{1,7},{2,4},{3,1},{4,6},{5,3},{6,0},{7,5},{8,10},{9,15},{10,... | collective-permute-start | bytes 786440 | tf_op jit(solution)/shard_map/ppermute | solution.py:378
  3.5 13.4 %collective-permute-start.1 = (bf16[32,4096]{1,0:T(8,128)(2,1)}, bf16[32,4096]{1,0:T(8,128)(2,1)S(1)}, u32[]{:S(2)}, u32[]{:S(2)}) collective-permute-start(bf16[32,4096]{1,0:T(8,128)(2,1)} %refs_0_.1), channel_id=1, source_target_pairs={{0,6},{1,3},{2,0},{3,5},{4,2},{5,7},{6,4},{7,1},{8,14},{9,11},{10,... | collective-permute-start | bytes 786440 | tf_op jit(solution)/shard_map/ppermute | solution.py:378
  7.1 11.3 %collective-permute-start = (bf16[32,4096]{1,0:T(8,128)(2,1)}, bf16[32,4096]{1,0:T(8,128)(2,1)}, u32[]{:S(2)}, u32[]{:S(2)}) collective-permute-start(bf16[32,4096]{1,0:T(8,128)(2,1)} %refs_0_.1), channel_id=1, source_target_pairs={{0,8},{1,9},{2,10},{3,11},{4,12},{5,13},{6,14},{7,15},{8,0},{9,1},... | collective-permute-start | bytes 786440 | tf_op jit(solution)/shard_map/ppermute | solution.py:378
  10.4 9.6 %collective-permute-start.3 = (bf16[32,4096]{1,0:T(8,128)(2,1)S(1)}, bf16[32,4096]{1,0:T(8,128)(2,1)}, u32[]{:S(2)}, u32[]{:S(2)}) collective-permute-start(bf16[32,4096]{1,0:T(8,128)(2,1)S(1)} %collective-permute-done.2.refs_1_), channel_id=1, source_target_pairs={{0,2},{1,7},{2,4},{3,1},{4,6},{5,3},{6,0},{7,5},{8,10},{9,15},{10,... | collective-permute-start | bytes 786440 | tf_op jit(solution)/shard_map/ppermute | solution.py:378
  13.0 0.8 copy-start.1
  13.9 18.1 %copy-start.6 = (s32[512]{0:T(512)S(1)}, s32[512]{0:T(512)}, u32[]{:S(2)}) copy-start(s32[512]{0:T(512)} %param.9) | copy-start | bytes 6148
  16.9 0.7 copy-start.4
  20.0 18.5 %collective-permute-start.4 = (bf16[256,4096]{1,0:T(8,128)(2,1)}, bf16[256,4096]{1,0:T(8,128)(2,1)}, u32[]{:S(2)}, u32[]{:S(2)}) collective-permute-start(bf16[256,4096]{1,0:T(8,128)(2,1)} %wave.1), channel_id=1, source_target_pairs={{0,1},{1,0},{2,3},{3,2},{4,5},{5,4},{6,7},{7,6},{8,9},{9,8},{10,11... | collective-permute-start | bytes 6291464 | tf_op jit(solution)/shard_map/ppermute | solution.py:378
  21.9 12.8 %collective-permute-start.7 = (bf16[32,4096]{1,0:T(8,128)(2,1)}, bf16[32,4096]{1,0:T(8,128)(2,1)}, u32[]{:S(2)}, u32[]{:S(2)}) collective-permute-start(bf16[32,4096]{1,0:T(8,128)(2,1)} %collective-permute-done.3.refs_3_), channel_id=1, source_target_pairs={{0,8},{1,9},{2,10},{3,11},{4,12},{5,13},{6,14},{7,15},{8,0},{9,1},... | collective-permute-start | bytes 786440 | tf_op jit(solution)/shard_map/ppermute | solution.py:378
  25.9 10.2 %collective-permute-start.6 = (bf16[32,4096]{1,0:T(8,128)(2,1)}, bf16[32,4096]{1,0:T(8,128)(2,1)}, u32[]{:S(2)}, u32[]{:S(2)}) collective-permute-start(bf16[32,4096]{1,0:T(8,128)(2,1)} %collective-permute-done.refs_4_), channel_id=1, source_target_pairs={{0,6},{1,3},{2,0},{3,5},{4,2},{5,7},{6,4},{7,1},{8,14},{9,11},{10,... | collective-permute-start | bytes 786440 | tf_op jit(solution)/shard_map/ppermute | solution.py:378
  28.7 9.8 %collective-permute-start.5 = (bf16[32,4096]{1,0:T(8,128)(2,1)}, bf16[32,4096]{1,0:T(8,128)(2,1)}, u32[]{:S(2)}, u32[]{:S(2)}) collective-permute-start(bf16[32,4096]{1,0:T(8,128)(2,1)} %collective-permute-done.refs_4_), channel_id=1, source_target_pairs={{0,2},{1,7},{2,4},{3,1},{4,6},{5,3},{6,0},{7,5},{8,10},{9,15},{10,... | collective-permute-start | bytes 786440 | tf_op jit(solution)/shard_map/ppermute | solution.py:378
  31.9 6.6 %copy-start.3 = (bf16[32,4096]{1,0:T(8,128)(2,1)S(1)}, bf16[32,4096]{1,0:T(8,128)(2,1)}, u32[]{:S(2)}) copy-start(bf16[32,4096]{1,0:T(8,128)(2,1)} %refs_0_.1) | copy-start | bytes 786436
  31.9 6.6 %copy-start.5 = (bf16[32,4096]{1,0:T(8,128)(2,1)S(1)}, bf16[32,4096]{1,0:T(8,128)(2,1)}, u32[]{:S(2)}) copy-start(bf16[32,4096]{1,0:T(8,128)(2,1)} %copy-done.4) | copy-start | bytes 786436
  41.9 0.7 copy-start
  42.6 60.5 %copy-start.2 = (s32[3,4096]{1,0:T(4,128)S(1)}, s32[3,4096]{1,0:T(4,128)}, u32[]{:S(2)}) copy-start(s32[3,4096]{1,0:T(4,128)} %gvec.3) | copy-start | bytes 147460
  42.6 16.7 %all-to-all-start = ((bf16[8,72,256]{2,1,0:T(8,128)(2,1)}), bf16[8,72,256]{2,1,0:T(8,128)(2,1)S(1)}, u32[]{:S(2)}, u32[]{:S(2)}) async-start(bf16[8,72,256]{2,1,0:T(8,128)(2,1)} %bitcast.20), calls=%async_computation | async-start | bytes 589824 | tf_op jit(solution)/shard_map/all_to_all | solution.py:399
  50.2 44.3 %collective-permute-start.8 = (bf16[256,4096]{1,0:T(8,128)(2,1)}, bf16[256,4096]{1,0:T(8,128)(2,1)}, u32[]{:S(2)}, u32[]{:S(2)}) collective-permute-start(bf16[256,4096]{1,0:T(8,128)(2,1)} %get-tuple-element.32.whole_own), channel_id=1, source_target_pairs={{0,1},{1,0},{2,3},{3,2},{4,5},{5,4},{6,7},{7,6},{8,9},{9,8},{10,11... | collective-permute-start | bytes 6291464 | tf_op jit(solution)/shard_map/ppermute | solution.py:378
  89.2 14.0 %all-to-all-start.2 = ((bf16[8,72,256]{2,1,0:T(8,128)(2,1)}), bf16[8,72,256]{2,1,0:T(8,128)(2,1)S(1)}, u32[]{:S(2)}, u32[]{:S(2)}) async-start(bf16[8,72,256]{2,1,0:T(8,128)(2,1)} %bitcast.15), calls=%async_computation.2 | async-start | bytes 589824 | tf_op jit(solution)/shard_map/all_to_all | solution.py:399

commit v3 on v2

--- a/solution.py
+++ b/solution.py
@@ -310,15 +310,18 @@
             energy = jnp.concatenate([energy_v[rows, :]] * (TILE // 128), axis=1)
             scale = jnp.concatenate([scale_v[rows, :]] * (TILE // 128), axis=1)
             resid = (kin - energy) * wave[rows, cols].astype(f32) + expanded_v[rows, :]
-            u = kin * scale
-            v = u * u
-            num = (1.0 + u) * (1.0 + v)
-            inverse = pl.reciprocal(num + 3.0 * (v * v), approx=True)
+            t = kin * scale
+            square = t * t
+            num = (3.0 + t) * (9.0 + square)
+            inverse = pl.reciprocal(num + square * square, approx=True)
             out_v[rows, cols] = ((num * inverse) * resid).astype(bf16)
 
-    for tile in range(N_TILES):
-        for copy in copies(tile):
-            copy.start()
+    def depart(tiles):
+        for tile in tiles:
+            for copy in copies(tile):
+                copy.start()
+
+    depart(range(3))
     core = place[CORE]
     blocks = coupled[...].astype(f32).reshape(NEAR, NEAR_ROWS, HALF_PROJ)
     for n in range(NEAR):
@@ -328,7 +331,8 @@
         halves_v[rows, HALF_PROJ:] = jnp.where(core == 0, second, first)
         energy, ekin = from_rows(blocks[n, 2 * BANDS:])
         energy_v[rows, :] = jnp.broadcast_to(energy, (BANDS, 128))
-        scale_v[rows, :] = jnp.broadcast_to((2.0 / 3.0) / ekin, (BANDS, 128))
+        scale_v[rows, :] = jnp.broadcast_to(2.0 / ekin, (BANDS, 128))
+    depart(range(3, N_TILES))
     arrive(0)
     expand(0, even_v)
 

time: 110 us -> 110 us (level)
  no operation moved by 1% of the time
where the time goes in v3:
time: 110 us; the launch traced here: 109 us
  starting transfers between devices  39.5 us (36%)
  blocking collectives  27.3 us (25%)
  waiting for transfers between devices  22 us (20%)
  Pallas kernels  17.5 us (16%)
  local copies, waits for them, and re-layouts  2.35 us (2%)
    all_to_all x1, blocking collectives, far_exchange(): lax.all_to_all(value, ('coef', 'band'), 0, 0, axis_index_groups=groups, t...  27.3 us
    ppermute x9, starting transfers between devices, along_band(): return lax.ppermute(value, 'band', band_perm(move))  26.7 us
    all_to_all x2, waiting for transfers between devices, near_exchange(): lax.all_to_all(value, 'coef', 0, 0, axis_index_groups=groups, tiled=True)  15.9 us
    all_to_all x2, starting transfers between devices, near_exchange(): lax.all_to_all(value, 'coef', 0, 0, axis_index_groups=groups, tiled=True)  12.9 us
    ppermute x9, waiting for transfers between devices, along_band(): return lax.ppermute(value, 'band', band_perm(move))  6.16 us
    pallas_call x1, Pallas kernels, finish(): pl.pallas_call(finish_kernel, in_specs=[smem] + [vmem] * 3 + [anywhere] *...  5.8 us
    pallas_call x1, Pallas kernels, intersect(): pl.pallas_call(intersect_kernel, in_specs=[smem] + [vmem] * (3 + N_SHARDS...  3.36 us
    pallas_call x1, Pallas kernels, stats(): pl.pallas_call(stats_kernel, in_specs=[anywhere, vmem], out_specs=[vmem,...  3.04 us
  transfers between devices with their start and end apart: 11, of which 6 were waited for; matrix products, arithmetic and copies ran while one was open for 0% of the time, Pallas kernels for 8%

profile of v3, /device:TPU:6, one launch (start us, length us, event | category | flops | bytes accessed | tf_op | source)
XLA Modules:
  0.0 108.9 jit_solution(11695546619308603748)
XLA Ops:
  0.0 3.5 %collective-permute-start.2 = (bf16[32,4096]{1,0:T(8,128)(2,1)}, bf16[32,4096]{1,0:T(8,128)(2,1)S(1)}, u32[]{:S(2)}, u32[]{:S(2)}) collective-permute-start(bf16[32,4096]{1,0:T(8,128)(2,1)} %refs_0_.1), channel_id=1, source_target_pairs={{0,2},{1,7},{2,4},{3,1},{4,6},{5,3},{6,0},{7,5},{8,10},{9,15},{10,... | collective-permute-start | bytes 786440 | tf_op jit(solution)/shard_map/ppermute | solution.py:382
  3.5 3.6 %collective-permute-start.1 = (bf16[32,4096]{1,0:T(8,128)(2,1)}, bf16[32,4096]{1,0:T(8,128)(2,1)S(1)}, u32[]{:S(2)}, u32[]{:S(2)}) collective-permute-start(bf16[32,4096]{1,0:T(8,128)(2,1)} %refs_0_.1), channel_id=1, source_target_pairs={{0,6},{1,3},{2,0},{3,5},{4,2},{5,7},{6,4},{7,1},{8,14},{9,11},{10,... | collective-permute-start | bytes 786440 | tf_op jit(solution)/shard_map/ppermute | solution.py:382
  7.1 3.3 %collective-permute-start = (bf16[32,4096]{1,0:T(8,128)(2,1)}, bf16[32,4096]{1,0:T(8,128)(2,1)}, u32[]{:S(2)}, u32[]{:S(2)}) collective-permute-start(bf16[32,4096]{1,0:T(8,128)(2,1)} %refs_0_.1), channel_id=1, source_target_pairs={{0,8},{1,9},{2,10},{3,11},{4,12},{5,13},{6,14},{7,15},{8,0},{9,1},... | collective-permute-start | bytes 786440 | tf_op jit(solution)/shard_map/ppermute | solution.py:382
  10.4 0.0 collective-permute-done.2.refs_1_
  10.4 2.6 %collective-permute-start.3 = (bf16[32,4096]{1,0:T(8,128)(2,1)S(1)}, bf16[32,4096]{1,0:T(8,128)(2,1)}, u32[]{:S(2)}, u32[]{:S(2)}) collective-permute-start(bf16[32,4096]{1,0:T(8,128)(2,1)S(1)} %collective-permute-done.2.refs_1_), channel_id=1, source_target_pairs={{0,2},{1,7},{2,4},{3,1},{4,6},{5,3},{6,0},{7,5},{8,10},{9,15},{10,... | collective-permute-start | bytes 786440 | tf_op jit(solution)/shard_map/ppermute | solution.py:382
  13.0 0.0 copy-start.1
  13.0 0.8 copy-done.1
  13.9 0.0 copy-start.6
  13.9 3.0 %stats.1 = (f32[64,256]{1,0:T(8,128)S(1)}, bf16[256,4096]{1,0:T(8,128)(2,1)S(1)}) custom-call(bf16[256,4096]{1,0:T(8,128)(2,1)} %wave.1, s32[3,4096]{1,0:T(4,128)S(1)} %copy-done.1), custom_call_target="tpu_custom_call" | custom-call | flops 5242880 | bytes 2097152 | tf_op jit(solution)/shard_map/stats/pallas_call | solution.py:118
  16.9 0.0 collective-permute-done.1.refs_2_
  16.9 0.0 copy-start.4
  16.9 0.7 copy-done.4
  17.6 0.7 collective-permute-done.refs_4_
  18.3 1.6 %collective-permute-done.3.refs_3_ = bf16[32,4096]{1,0:T(8,128)(2,1)} collective-permute-done((bf16[32,4096]{1,0:T(8,128)(2,1)S(1)}, bf16[32,4096]{1,0:T(8,128)(2,1)}, u32[]{:S(2)}, u32[]{:S(2)}) %collective-permute-start.3) | collective-permute-done | bytes 262176 | tf_op jit(solution)/shard_map/ppermute | solution.py:382
  20.0 1.9 %collective-permute-start.4 = (bf16[256,4096]{1,0:T(8,128)(2,1)}, bf16[256,4096]{1,0:T(8,128)(2,1)}, u32[]{:S(2)}, u32[]{:S(2)}) collective-permute-start(bf16[256,4096]{1,0:T(8,128)(2,1)} %wave.1), channel_id=1, source_target_pairs={{0,1},{1,0},{2,3},{3,2},{4,5},{5,4},{6,7},{7,6},{8,9},{9,8},{10,11... | collective-permute-start | bytes 6291464 | tf_op jit(solution)/shard_map/ppermute | solution.py:382
  21.9 4.0 %collective-permute-start.7 = (bf16[32,4096]{1,0:T(8,128)(2,1)}, bf16[32,4096]{1,0:T(8,128)(2,1)}, u32[]{:S(2)}, u32[]{:S(2)}) collective-permute-start(bf16[32,4096]{1,0:T(8,128)(2,1)} %collective-permute-done.3.refs_3_), channel_id=1, source_target_pairs={{0,8},{1,9},{2,10},{3,11},{4,12},{5,13},{6,14},{7,15},{8,0},{9,1},... | collective-permute-start | bytes 786440 | tf_op jit(solution)/shard_map/ppermute | solution.py:382
  25.9 2.8 %collective-permute-start.6 = (bf16[32,4096]{1,0:T(8,128)(2,1)}, bf16[32,4096]{1,0:T(8,128)(2,1)}, u32[]{:S(2)}, u32[]{:S(2)}) collective-permute-start(bf16[32,4096]{1,0:T(8,128)(2,1)} %collective-permute-done.refs_4_), channel_id=1, source_target_pairs={{0,6},{1,3},{2,0},{3,5},{4,2},{5,7},{6,4},{7,1},{8,14},{9,11},{10,... | collective-permute-start | bytes 786440 | tf_op jit(solution)/shard_map/ppermute | solution.py:382
  28.7 3.1 %collective-permute-start.5 = (bf16[32,4096]{1,0:T(8,128)(2,1)}, bf16[32,4096]{1,0:T(8,128)(2,1)}, u32[]{:S(2)}, u32[]{:S(2)}) collective-permute-start(bf16[32,4096]{1,0:T(8,128)(2,1)} %collective-permute-done.refs_4_), channel_id=1, source_target_pairs={{0,2},{1,7},{2,4},{3,1},{4,6},{5,3},{6,0},{7,5},{8,10},{9,15},{10,... | collective-permute-start | bytes 786440 | tf_op jit(solution)/shard_map/ppermute | solution.py:382
  31.8 0.1 stack.43.place
  31.9 0.0 copy-done.6
  31.9 0.0 copy-start.3
  31.9 0.0 copy-start.5
  31.9 2.8 %masked_weights.1.weights = bf16[512,1024]{1,0:T(8,128)(2,1)S(1)} custom-call(s32[1,512]{1,0:T(1,128)S(1)} %bitcast.22, bf16[512,512]{1,0:T(8,128)(2,1)} %dion, bf16[512,512]{1,0:T(8,128)(2,1)} %qaug.1), custom_call_target="tpu_custom_call" | custom-call | flops 1207959552 | bytes 2097152 | tf_op jit(solution)/shard_map/masked_weights/pallas_call | solution.py:148
  34.7 0.0 collective-permute-done.7.refs_7_
  34.7 1.4 %collective-permute-done.6.refs_6_ = bf16[32,4096]{1,0:T(8,128)(2,1)} collective-permute-done((bf16[32,4096]{1,0:T(8,128)(2,1)}, bf16[32,4096]{1,0:T(8,128)(2,1)}, u32[]{:S(2)}, u32[]{:S(2)}) %collective-permute-start.6) | collective-permute-done | bytes 262176 | tf_op jit(solution)/shard_map/ppermute | solution.py:382
  36.1 2.4 %collective-permute-done.5.refs_5_ = bf16[32,4096]{1,0:T(8,128)(2,1)} collective-permute-done((bf16[32,4096]{1,0:T(8,128)(2,1)}, bf16[32,4096]{1,0:T(8,128)(2,1)}, u32[]{:S(2)}, u32[]{:S(2)}) %collective-permute-start.5) | collective-permute-done | bytes 262176 | tf_op jit(solution)/shard_map/ppermute | solution.py:382
  38.5 0.0 collective-permute-done.4.wave_other
  38.5 0.0 copy-done.3
  38.5 0.0 copy-done.5
  38.5 3.4 %intersect.1 = (bf16[576,256]{1,0:T(8,128)(2,1)S(1)}, bf16[256,4096]{1,0:T(8,128)(2,1)}) custom-call(s32[10]{0:T(128)S(1)} %stack.43.place, f32[64,256]{1,0:T(8,128)S(1)} %get-tuple-element.22.stat, bf16[256,4096]{1,0:T(8,128)(2,1)S(1)} %get-tuple-element.23.wave_own.wave, bf16[256,4096]{1,0:T(8,128)(2,1)} %collective-permute-done.4.wave_other, ...), custom_call_target="tpu_custom_call" | custom-call | flops 1073741824 | bytes 8388608 | tf_op jit(solution)/shard_map/intersect/pallas_call | solution.py:187
  41.9 0.0 copy-start
  41.9 0.7 copy-done
  42.6 0.0 copy-start.2
  42.6 7.6 %all-to-all-start = ((bf16[8,72,256]{2,1,0:T(8,128)(2,1)}), bf16[8,72,256]{2,1,0:T(8,128)(2,1)S(1)}, u32[]{:S(2)}, u32[]{:S(2)}) async-start(bf16[8,72,256]{2,1,0:T(8,128)(2,1)} %bitcast.20), calls=%async_computation | async-start | bytes 589824 | tf_op jit(solution)/shard_map/all_to_all | solution.py:403
  50.2 1.9 %collective-permute-start.8 = (bf16[256,4096]{1,0:T(8,128)(2,1)}, bf16[256,4096]{1,0:T(8,128)(2,1)}, u32[]{:S(2)}, u32[]{:S(2)}) collective-permute-start(bf16[256,4096]{1,0:T(8,128)(2,1)} %get-tuple-element.32.whole_own), channel_id=1, source_target_pairs={{0,1},{1,0},{2,3},{3,2},{4,5},{5,4},{6,7},{7,6},{8,9},{9,8},{10,11... | collective-permute-start | bytes 6291464 | tf_op jit(solution)/shard_map/ppermute | solution.py:382
  52.1 7.2 %all-to-all-done = bf16[8,72,256]{2,1,0:T(8,128)(2,1)S(1)} async-done(((bf16[8,72,256]{2,1,0:T(8,128)(2,1)}), bf16[8,72,256]{2,1,0:T(8,128)(2,1)S(1)}, u32[]{:S(2)}, u32[]{:S(2)}) %all-to-all-start) | async-done | bytes 294944 | tf_op jit(solution)/shard_map/all_to_all | solution.py:403
  59.3 0.7 near_sum.1
  60.0 27.3 %all_to_all.33 = bf16[8,40,256]{2,1,0:T(8,128)(2,1)S(1)} all-to-all(bf16[8,40,256]{2,1,0:T(8,128)(2,1)S(1)} %bitcast.21), channel_id=1, replica_groups={{0,1,128,129,256,257,384,385},{2,3,130,131,258,259,386,387},{4,5,132,13..., dimensions={0} | all-to-all | bytes 327680 | tf_op jit(solution)/shard_map/all_to_all | solution.py:411
  87.4 1.8 %couple.1 = bf16[576,256]{1,0:T(8,128)(2,1)} custom-call(s32[10]{0:T(128)S(1)} %stack.43.place, f32[32,256]{1,0:T(8,128)S(1)} %get-tuple-element.29.keep, bf16[320,256]{1,0:T(8,128)(2,1)S(1)} %bitcast.19, bf16[512,1024]{1,0:T(8,128)(2,1)S(1)} %masked_weights.1.weights), custom_call_target="tpu_custom_call" | custom-call | flops 100663296 | bytes 1572864 | tf_op jit(solution)/shard_map/couple/pallas_call | solution.py:264
  89.2 5.3 %all-to-all-start.2 = ((bf16[8,72,256]{2,1,0:T(8,128)(2,1)}), bf16[8,72,256]{2,1,0:T(8,128)(2,1)S(1)}, u32[]{:S(2)}, u32[]{:S(2)}) async-start(bf16[8,72,256]{2,1,0:T(8,128)(2,1)} %bitcast.15), calls=%async_computation.2 | async-start | bytes 589824 | tf_op jit(solution)/shard_map/all_to_all | solution.py:403
  94.5 0.0 collective-permute-done.8.whole_other
  94.5 8.7 %all-to-all-done.2 = bf16[8,72,256]{2,1,0:T(8,128)(2,1)S(1)} async-done(((bf16[8,72,256]{2,1,0:T(8,128)(2,1)}), bf16[8,72,256]{2,1,0:T(8,128)(2,1)S(1)}, u32[]{:S(2)}, u32[]{:S(2)}) %all-to-all-start.2) | async-done | bytes 294944 | tf_op jit(solution)/shard_map/all_to_all | solution.py:403
  103.1 0.0 copy-done.2
  103.1 5.8 %finish.1 = bf16[256,4096]{1,0:T(8,128)(2,1)} custom-call(s32[10]{0:T(128)S(1)} %stack.43.place, bf16[576,256]{1,0:T(8,128)(2,1)S(1)} %bitcast.17, s32[3,4096]{1,0:T(4,128)S(1)} %copy-done.2, bf16[256,4096]{1,0:T(8,128)(2,1)S(1)} %get-tuple-element.23.wave_own.wave, bf16[256,4096]{1,0:T(8,128)(2,1)} %get-tuple-element.32.whole_own, ...), custom_call_target="tpu_custom_call" | custom-call | flops 1073741824 | bytes 8388608 | tf_op jit(solution)/shard_map/finish/pallas_call | solution.py:359
Async XLA Ops:
  0.0 10.4 %collective-permute-start.2 = (bf16[32,4096]{1,0:T(8,128)(2,1)}, bf16[32,4096]{1,0:T(8,128)(2,1)S(1)}, u32[]{:S(2)}, u32[]{:S(2)}) collective-permute-start(bf16[32,4096]{1,0:T(8,128)(2,1)} %refs_0_.1), channel_id=1, source_target_pairs={{0,2},{1,7},{2,4},{3,1},{4,6},{5,3},{6,0},{7,5},{8,10},{9,15},{10,... | collective-permute-start | bytes 786440 | tf_op jit(solution)/shard_map/ppermute | solution.py:382
  3.5 13.4 %collective-permute-start.1 = (bf16[32,4096]{1,0:T(8,128)(2,1)}, bf16[32,4096]{1,0:T(8,128)(2,1)S(1)}, u32[]{:S(2)}, u32[]{:S(2)}) collective-permute-start(bf16[32,4096]{1,0:T(8,128)(2,1)} %refs_0_.1), channel_id=1, source_target_pairs={{0,6},{1,3},{2,0},{3,5},{4,2},{5,7},{6,4},{7,1},{8,14},{9,11},{10,... | collective-permute-start | bytes 786440 | tf_op jit(solution)/shard_map/ppermute | solution.py:382
  7.1 11.3 %collective-permute-start = (bf16[32,4096]{1,0:T(8,128)(2,1)}, bf16[32,4096]{1,0:T(8,128)(2,1)}, u32[]{:S(2)}, u32[]{:S(2)}) collective-permute-start(bf16[32,4096]{1,0:T(8,128)(2,1)} %refs_0_.1), channel_id=1, source_target_pairs={{0,8},{1,9},{2,10},{3,11},{4,12},{5,13},{6,14},{7,15},{8,0},{9,1},... | collective-permute-start | bytes 786440 | tf_op jit(solution)/shard_map/ppermute | solution.py:382
  10.4 9.6 %collective-permute-start.3 = (bf16[32,4096]{1,0:T(8,128)(2,1)S(1)}, bf16[32,4096]{1,0:T(8,128)(2,1)}, u32[]{:S(2)}, u32[]{:S(2)}) collective-permute-start(bf16[32,4096]{1,0:T(8,128)(2,1)S(1)} %collective-permute-done.2.refs_1_), channel_id=1, source_target_pairs={{0,2},{1,7},{2,4},{3,1},{4,6},{5,3},{6,0},{7,5},{8,10},{9,15},{10,... | collective-permute-start | bytes 786440 | tf_op jit(solution)/shard_map/ppermute | solution.py:382
  13.0 0.8 copy-start.1
  13.9 18.1 %copy-start.6 = (s32[512]{0:T(512)S(1)}, s32[512]{0:T(512)}, u32[]{:S(2)}) copy-start(s32[512]{0:T(512)} %param.9) | copy-start | bytes 6148
  16.9 0.7 copy-start.4
  20.0 18.5 %collective-permute-start.4 = (bf16[256,4096]{1,0:T(8,128)(2,1)}, bf16[256,4096]{1,0:T(8,128)(2,1)}, u32[]{:S(2)}, u32[]{:S(2)}) collective-permute-start(bf16[256,4096]{1,0:T(8,128)(2,1)} %wave.1), channel_id=1, source_target_pairs={{0,1},{1,0},{2,3},{3,2},{4,5},{5,4},{6,7},{7,6},{8,9},{9,8},{10,11... | collective-permute-start | bytes 6291464 | tf_op jit(solution)/shard_map/ppermute | solution.py:382
  21.9 12.8 %collective-permute-start.7 = (bf16[32,4096]{1,0:T(8,128)(2,1)}, bf16[32,4096]{1,0:T(8,128)(2,1)}, u32[]{:S(2)}, u32[]{:S(2)}) collective-permute-start(bf16[32,4096]{1,0:T(8,128)(2,1)} %collective-permute-done.3.refs_3_), channel_id=1, source_target_pairs={{0,8},{1,9},{2,10},{3,11},{4,12},{5,13},{6,14},{7,15},{8,0},{9,1},... | collective-permute-start | bytes 786440 | tf_op jit(solution)/shard_map/ppermute | solution.py:382
  25.9 10.2 %collective-permute-start.6 = (bf16[32,4096]{1,0:T(8,128)(2,1)}, bf16[32,4096]{1,0:T(8,128)(2,1)}, u32[]{:S(2)}, u32[]{:S(2)}) collective-permute-start(bf16[32,4096]{1,0:T(8,128)(2,1)} %collective-permute-done.refs_4_), channel_id=1, source_target_pairs={{0,6},{1,3},{2,0},{3,5},{4,2},{5,7},{6,4},{7,1},{8,14},{9,11},{10,... | collective-permute-start | bytes 786440 | tf_op jit(solution)/shard_map/ppermute | solution.py:382
  28.7 9.8 %collective-permute-start.5 = (bf16[32,4096]{1,0:T(8,128)(2,1)}, bf16[32,4096]{1,0:T(8,128)(2,1)}, u32[]{:S(2)}, u32[]{:S(2)}) collective-permute-start(bf16[32,4096]{1,0:T(8,128)(2,1)} %collective-permute-done.refs_4_), channel_id=1, source_target_pairs={{0,2},{1,7},{2,4},{3,1},{4,6},{5,3},{6,0},{7,5},{8,10},{9,15},{10,... | collective-permute-start | bytes 786440 | tf_op jit(solution)/shard_map/ppermute | solution.py:382
  31.9 6.6 %copy-start.3 = (bf16[32,4096]{1,0:T(8,128)(2,1)S(1)}, bf16[32,4096]{1,0:T(8,128)(2,1)}, u32[]{:S(2)}) copy-start(bf16[32,4096]{1,0:T(8,128)(2,1)} %refs_0_.1) | copy-start | bytes 786436
  31.9 6.6 %copy-start.5 = (bf16[32,4096]{1,0:T(8,128)(2,1)S(1)}, bf16[32,4096]{1,0:T(8,128)(2,1)}, u32[]{:S(2)}) copy-start(bf16[32,4096]{1,0:T(8,128)(2,1)} %copy-done.4) | copy-start | bytes 786436
  41.9 0.7 copy-start
  42.6 60.5 %copy-start.2 = (s32[3,4096]{1,0:T(4,128)S(1)}, s32[3,4096]{1,0:T(4,128)}, u32[]{:S(2)}) copy-start(s32[3,4096]{1,0:T(4,128)} %gvec.3) | copy-start | bytes 147460
  42.6 16.7 %all-to-all-start = ((bf16[8,72,256]{2,1,0:T(8,128)(2,1)}), bf16[8,72,256]{2,1,0:T(8,128)(2,1)S(1)}, u32[]{:S(2)}, u32[]{:S(2)}) async-start(bf16[8,72,256]{2,1,0:T(8,128)(2,1)} %bitcast.20), calls=%async_computation | async-start | bytes 589824 | tf_op jit(solution)/shard_map/all_to_all | solution.py:403
  50.2 44.3 %collective-permute-start.8 = (bf16[256,4096]{1,0:T(8,128)(2,1)}, bf16[256,4096]{1,0:T(8,128)(2,1)}, u32[]{:S(2)}, u32[]{:S(2)}) collective-permute-start(bf16[256,4096]{1,0:T(8,128)(2,1)} %get-tuple-element.32.whole_own), channel_id=1, source_target_pairs={{0,1},{1,0},{2,3},{3,2},{4,5},{5,4},{6,7},{7,6},{8,9},{9,8},{10,11... | collective-permute-start | bytes 6291464 | tf_op jit(solution)/shard_map/ppermute | solution.py:382
  89.2 14.0 %all-to-all-start.2 = ((bf16[8,72,256]{2,1,0:T(8,128)(2,1)}), bf16[8,72,256]{2,1,0:T(8,128)(2,1)S(1)}, u32[]{:S(2)}, u32[]{:S(2)}) async-start(bf16[8,72,256]{2,1,0:T(8,128)(2,1)} %bitcast.15), calls=%async_computation.2 | async-start | bytes 589824 | tf_op jit(solution)/shard_map/all_to_all | solution.py:403

commit v4 on v3

--- a/solution.py
+++ b/solution.py
@@ -280,7 +280,7 @@
 def finish_kernel(place, coupled, gvec, wave, whole_own, whole_other, out,
                   whole_v, out_v, halves_v, energy_v, scale_v, even_v, odd_v, sems, out_sems):
     def columns(tile):
-        return pl.ds(pl.multiple_of(tile * TILE, TILE), TILE)
+        return slice(tile * TILE, (tile + 1) * TILE)
 
     def copies(tile):
         cols = columns(tile)
@@ -336,20 +336,13 @@
     arrive(0)
     expand(0, even_v)
 
-    @pl.loop(0, N_TILES // 2)
-    def _(i):
-        arrive(2 * i + 1)
-
-        @pl.when(i + 1 < N_TILES // 2)
-        def _():
-            arrive(2 * i + 2)
-
-        expand(2 * i + 1, odd_v)
-        conclude(2 * i, even_v)
-        out_copy(2 * i).start()
-        expand(jnp.minimum(2 * i + 2, N_TILES - 1), even_v)
-        conclude(2 * i + 1, odd_v)
-        out_copy(2 * i + 1).start()
+    buffers = (even_v, odd_v)
+    for tile in range(N_TILES):
+        if tile + 1 < N_TILES:
+            arrive(tile + 1)
+            expand(tile + 1, buffers[(tile + 1) % 2])
+        conclude(tile, buffers[tile % 2])
+        out_copy(tile).start()
 
     for tile in range(N_TILES):
         out_copy(tile).wait()

time: 110 us -> 110 us (level)
  no operation moved by 1% of the time
where the time goes in v4:
time: 110 us
  starting transfers between devices  39.5 us (36%)
  blocking collectives  27.3 us (25%)
  waiting for transfers between devices  22 us (20%)
  Pallas kernels  18.1 us (16%)
  local copies, waits for them, and re-layouts  2.35 us (2%)
    all_to_all x1, blocking collectives, far_exchange(): lax.all_to_all(value, ('coef', 'band'), 0, 0, axis_index_groups=groups, t...  27.3 us
    ppermute x9, starting transfers between devices, along_band(): return lax.ppermute(value, 'band', band_perm(move))  26.7 us
    all_to_all x2, waiting for transfers between devices, near_exchange(): lax.all_to_all(value, 'coef', 0, 0, axis_index_groups=groups, tiled=True)  15.9 us
    all_to_all x2, starting transfers between devices, near_exchange(): lax.all_to_all(value, 'coef', 0, 0, axis_index_groups=groups, tiled=True)  12.9 us
    pallas_call x1, Pallas kernels, finish(): pl.pallas_call(finish_kernel, in_specs=[smem] + [vmem] * 3 + [anywhere] *...  6.38 us
    ppermute x9, waiting for transfers between devices, along_band(): return lax.ppermute(value, 'band', band_perm(move))  6.16 us
    pallas_call x1, Pallas kernels, intersect(): pl.pallas_call(intersect_kernel, in_specs=[smem] + [vmem] * (3 + N_SHARDS...  3.36 us
    pallas_call x1, Pallas kernels, stats(): pl.pallas_call(stats_kernel, in_specs=[anywhere, vmem], out_specs=[vmem,...  3.04 us
  transfers between devices with their start and end apart: 11, of which 6 were waited for; matrix products, arithmetic and copies ran while one was open for 0% of the time, Pallas kernels for 8%

profile of v4, /device:TPU:6, one launch (start us, length us, event | category | flops | bytes accessed | tf_op | source)
XLA Modules:
  0.0 109.5 jit_solution(9193764941454235326)
XLA Ops:
  0.0 3.5 %collective-permute-start.2 = (bf16[32,4096]{1,0:T(8,128)(2,1)}, bf16[32,4096]{1,0:T(8,128)(2,1)S(1)}, u32[]{:S(2)}, u32[]{:S(2)}) collective-permute-start(bf16[32,4096]{1,0:T(8,128)(2,1)} %refs_0_.1), channel_id=1, source_target_pairs={{0,2},{1,7},{2,4},{3,1},{4,6},{5,3},{6,0},{7,5},{8,10},{9,15},{10,... | collective-permute-start | bytes 786440 | tf_op jit(solution)/shard_map/ppermute | solution.py:375
  3.5 3.6 %collective-permute-start.1 = (bf16[32,4096]{1,0:T(8,128)(2,1)}, bf16[32,4096]{1,0:T(8,128)(2,1)S(1)}, u32[]{:S(2)}, u32[]{:S(2)}) collective-permute-start(bf16[32,4096]{1,0:T(8,128)(2,1)} %refs_0_.1), channel_id=1, source_target_pairs={{0,6},{1,3},{2,0},{3,5},{4,2},{5,7},{6,4},{7,1},{8,14},{9,11},{10,... | collective-permute-start | bytes 786440 | tf_op jit(solution)/shard_map/ppermute | solution.py:375
  7.1 3.3 %collective-permute-start = (bf16[32,4096]{1,0:T(8,128)(2,1)}, bf16[32,4096]{1,0:T(8,128)(2,1)}, u32[]{:S(2)}, u32[]{:S(2)}) collective-permute-start(bf16[32,4096]{1,0:T(8,128)(2,1)} %refs_0_.1), channel_id=1, source_target_pairs={{0,8},{1,9},{2,10},{3,11},{4,12},{5,13},{6,14},{7,15},{8,0},{9,1},... | collective-permute-start | bytes 786440 | tf_op jit(solution)/shard_map/ppermute | solution.py:375
  10.4 0.0 collective-permute-done.2.refs_1_
  10.4 2.6 %collective-permute-start.3 = (bf16[32,4096]{1,0:T(8,128)(2,1)S(1)}, bf16[32,4096]{1,0:T(8,128)(2,1)}, u32[]{:S(2)}, u32[]{:S(2)}) collective-permute-start(bf16[32,4096]{1,0:T(8,128)(2,1)S(1)} %collective-permute-done.2.refs_1_), channel_id=1, source_target_pairs={{0,2},{1,7},{2,4},{3,1},{4,6},{5,3},{6,0},{7,5},{8,10},{9,15},{10,... | collective-permute-start | bytes 786440 | tf_op jit(solution)/shard_map/ppermute | solution.py:375
  13.0 0.0 copy-start.1
  13.0 0.8 copy-done.1
  13.9 0.0 copy-start.6
  13.9 3.0 %stats.1 = (f32[64,256]{1,0:T(8,128)S(1)}, bf16[256,4096]{1,0:T(8,128)(2,1)S(1)}) custom-call(bf16[256,4096]{1,0:T(8,128)(2,1)} %wave.1, s32[3,4096]{1,0:T(4,128)S(1)} %copy-done.1), custom_call_target="tpu_custom_call" | custom-call | flops 5242880 | bytes 2097152 | tf_op jit(solution)/shard_map/stats/pallas_call | solution.py:118
  16.9 0.0 collective-permute-done.1.refs_2_
  16.9 0.0 copy-start.4
  16.9 0.7 copy-done.4
  17.6 0.7 collective-permute-done.refs_4_
  18.3 1.6 %collective-permute-done.3.refs_3_ = bf16[32,4096]{1,0:T(8,128)(2,1)} collective-permute-done((bf16[32,4096]{1,0:T(8,128)(2,1)S(1)}, bf16[32,4096]{1,0:T(8,128)(2,1)}, u32[]{:S(2)}, u32[]{:S(2)}) %collective-permute-start.3) | collective-permute-done | bytes 262176 | tf_op jit(solution)/shard_map/ppermute | solution.py:375
  20.0 1.9 %collective-permute-start.4 = (bf16[256,4096]{1,0:T(8,128)(2,1)}, bf16[256,4096]{1,0:T(8,128)(2,1)}, u32[]{:S(2)}, u32[]{:S(2)}) collective-permute-start(bf16[256,4096]{1,0:T(8,128)(2,1)} %wave.1), channel_id=1, source_target_pairs={{0,1},{1,0},{2,3},{3,2},{4,5},{5,4},{6,7},{7,6},{8,9},{9,8},{10,11... | collective-permute-start | bytes 6291464 | tf_op jit(solution)/shard_map/ppermute | solution.py:375
  21.9 4.0 %collective-permute-start.7 = (bf16[32,4096]{1,0:T(8,128)(2,1)}, bf16[32,4096]{1,0:T(8,128)(2,1)}, u32[]{:S(2)}, u32[]{:S(2)}) collective-permute-start(bf16[32,4096]{1,0:T(8,128)(2,1)} %collective-permute-done.3.refs_3_), channel_id=1, source_target_pairs={{0,8},{1,9},{2,10},{3,11},{4,12},{5,13},{6,14},{7,15},{8,0},{9,1},... | collective-permute-start | bytes 786440 | tf_op jit(solution)/shard_map/ppermute | solution.py:375
  25.9 2.8 %collective-permute-start.6 = (bf16[32,4096]{1,0:T(8,128)(2,1)}, bf16[32,4096]{1,0:T(8,128)(2,1)}, u32[]{:S(2)}, u32[]{:S(2)}) collective-permute-start(bf16[32,4096]{1,0:T(8,128)(2,1)} %collective-permute-done.refs_4_), channel_id=1, source_target_pairs={{0,6},{1,3},{2,0},{3,5},{4,2},{5,7},{6,4},{7,1},{8,14},{9,11},{10,... | collective-permute-start | bytes 786440 | tf_op jit(solution)/shard_map/ppermute | solution.py:375
  28.7 3.1 %collective-permute-start.5 = (bf16[32,4096]{1,0:T(8,128)(2,1)}, bf16[32,4096]{1,0:T(8,128)(2,1)}, u32[]{:S(2)}, u32[]{:S(2)}) collective-permute-start(bf16[32,4096]{1,0:T(8,128)(2,1)} %collective-permute-done.refs_4_), channel_id=1, source_target_pairs={{0,2},{1,7},{2,4},{3,1},{4,6},{5,3},{6,0},{7,5},{8,10},{9,15},{10,... | collective-permute-start | bytes 786440 | tf_op jit(solution)/shard_map/ppermute | solution.py:375
  31.8 0.1 stack.43.place
  31.9 0.0 copy-done.6
  31.9 0.0 copy-start.3
  31.9 0.0 copy-start.5
  31.9 2.8 %masked_weights.1.weights = bf16[512,1024]{1,0:T(8,128)(2,1)S(1)} custom-call(s32[1,512]{1,0:T(1,128)S(1)} %bitcast.22, bf16[512,512]{1,0:T(8,128)(2,1)} %dion, bf16[512,512]{1,0:T(8,128)(2,1)} %qaug.1), custom_call_target="tpu_custom_call" | custom-call | flops 1207959552 | bytes 2097152 | tf_op jit(solution)/shard_map/masked_weights/pallas_call | solution.py:148
  34.7 0.0 collective-permute-done.7.refs_7_
  34.7 1.4 %collective-permute-done.6.refs_6_ = bf16[32,4096]{1,0:T(8,128)(2,1)} collective-permute-done((bf16[32,4096]{1,0:T(8,128)(2,1)}, bf16[32,4096]{1,0:T(8,128)(2,1)}, u32[]{:S(2)}, u32[]{:S(2)}) %collective-permute-start.6) | collective-permute-done | bytes 262176 | tf_op jit(solution)/shard_map/ppermute | solution.py:375
  36.1 2.4 %collective-permute-done.5.refs_5_ = bf16[32,4096]{1,0:T(8,128)(2,1)} collective-permute-done((bf16[32,4096]{1,0:T(8,128)(2,1)}, bf16[32,4096]{1,0:T(8,128)(2,1)}, u32[]{:S(2)}, u32[]{:S(2)}) %collective-permute-start.5) | collective-permute-done | bytes 262176 | tf_op jit(solution)/shard_map/ppermute | solution.py:375
  38.5 0.0 collective-permute-done.4.wave_other
  38.5 0.0 copy-done.3
  38.5 0.0 copy-done.5
  38.5 3.4 %intersect.1 = (bf16[576,256]{1,0:T(8,128)(2,1)S(1)}, bf16[256,4096]{1,0:T(8,128)(2,1)}) custom-call(s32[10]{0:T(128)S(1)} %stack.43.place, f32[64,256]{1,0:T(8,128)S(1)} %get-tuple-element.22.stat, bf16[256,4096]{1,0:T(8,128)(2,1)S(1)} %get-tuple-element.23.wave_own.wave, bf16[256,4096]{1,0:T(8,128)(2,1)} %collective-permute-done.4.wave_other, ...), custom_call_target="tpu_custom_call" | custom-call | flops 1073741824 | bytes 8388608 | tf_op jit(solution)/shard_map/intersect/pallas_call | solution.py:187
  41.9 0.0 copy-start
  41.9 0.7 copy-done
  42.6 0.0 copy-start.2
  42.6 7.6 %all-to-all-start = ((bf16[8,72,256]{2,1,0:T(8,128)(2,1)}), bf16[8,72,256]{2,1,0:T(8,128)(2,1)S(1)}, u32[]{:S(2)}, u32[]{:S(2)}) async-start(bf16[8,72,256]{2,1,0:T(8,128)(2,1)} %bitcast.20), calls=%async_computation | async-start | bytes 589824 | tf_op jit(solution)/shard_map/all_to_all | solution.py:396
  50.2 1.9 %collective-permute-start.8 = (bf16[256,4096]{1,0:T(8,128)(2,1)}, bf16[256,4096]{1,0:T(8,128)(2,1)}, u32[]{:S(2)}, u32[]{:S(2)}) collective-permute-start(bf16[256,4096]{1,0:T(8,128)(2,1)} %get-tuple-element.32.whole_own), channel_id=1, source_target_pairs={{0,1},{1,0},{2,3},{3,2},{4,5},{5,4},{6,7},{7,6},{8,9},{9,8},{10,11... | collective-permute-start | bytes 6291464 | tf_op jit(solution)/shard_map/ppermute | solution.py:375
  52.1 7.2 %all-to-all-done = bf16[8,72,256]{2,1,0:T(8,128)(2,1)S(1)} async-done(((bf16[8,72,256]{2,1,0:T(8,128)(2,1)}), bf16[8,72,256]{2,1,0:T(8,128)(2,1)S(1)}, u32[]{:S(2)}, u32[]{:S(2)}) %all-to-all-start) | async-done | bytes 294944 | tf_op jit(solution)/shard_map/all_to_all | solution.py:396
  59.3 0.7 near_sum.1
  60.0 27.3 %all_to_all.33 = bf16[8,40,256]{2,1,0:T(8,128)(2,1)S(1)} all-to-all(bf16[8,40,256]{2,1,0:T(8,128)(2,1)S(1)} %bitcast.21), channel_id=1, replica_groups={{0,1,128,129,256,257,384,385},{2,3,130,131,258,259,386,387},{4,5,132,13..., dimensions={0} | all-to-all | bytes 327680 | tf_op jit(solution)/shard_map/all_to_all | solution.py:404
  87.4 1.8 %couple.1 = bf16[576,256]{1,0:T(8,128)(2,1)} custom-call(s32[10]{0:T(128)S(1)} %stack.43.place, f32[32,256]{1,0:T(8,128)S(1)} %get-tuple-element.29.keep, bf16[320,256]{1,0:T(8,128)(2,1)S(1)} %bitcast.19, bf16[512,1024]{1,0:T(8,128)(2,1)S(1)} %masked_weights.1.weights), custom_call_target="tpu_custom_call" | custom-call | flops 100663296 | bytes 1572864 | tf_op jit(solution)/shard_map/couple/pallas_call | solution.py:264
  89.2 5.3 %all-to-all-start.2 = ((bf16[8,72,256]{2,1,0:T(8,128)(2,1)}), bf16[8,72,256]{2,1,0:T(8,128)(2,1)S(1)}, u32[]{:S(2)}, u32[]{:S(2)}) async-start(bf16[8,72,256]{2,1,0:T(8,128)(2,1)} %bitcast.15), calls=%async_computation.2 | async-start | bytes 589824 | tf_op jit(solution)/shard_map/all_to_all | solution.py:396
  94.5 0.0 collective-permute-done.8.whole_other
  94.5 8.7 %all-to-all-done.2 = bf16[8,72,256]{2,1,0:T(8,128)(2,1)S(1)} async-done(((bf16[8,72,256]{2,1,0:T(8,128)(2,1)}), bf16[8,72,256]{2,1,0:T(8,128)(2,1)S(1)}, u32[]{:S(2)}, u32[]{:S(2)}) %all-to-all-start.2) | async-done | bytes 294944 | tf_op jit(solution)/shard_map/all_to_all | solution.py:396
  103.1 0.0 copy-done.2
  103.1 6.4 %finish.1 = bf16[256,4096]{1,0:T(8,128)(2,1)} custom-call(s32[10]{0:T(128)S(1)} %stack.43.place, bf16[576,256]{1,0:T(8,128)(2,1)S(1)} %bitcast.17, s32[3,4096]{1,0:T(4,128)S(1)} %copy-done.2, bf16[256,4096]{1,0:T(8,128)(2,1)S(1)} %get-tuple-element.23.wave_own.wave, bf16[256,4096]{1,0:T(8,128)(2,1)} %get-tuple-element.32.whole_own, ...), custom_call_target="tpu_custom_call" | custom-call | flops 1073741824 | bytes 8388608 | tf_op jit(solution)/shard_map/finish/pallas_call | solution.py:352
Async XLA Ops:
  0.0 10.4 %collective-permute-start.2 = (bf16[32,4096]{1,0:T(8,128)(2,1)}, bf16[32,4096]{1,0:T(8,128)(2,1)S(1)}, u32[]{:S(2)}, u32[]{:S(2)}) collective-permute-start(bf16[32,4096]{1,0:T(8,128)(2,1)} %refs_0_.1), channel_id=1, source_target_pairs={{0,2},{1,7},{2,4},{3,1},{4,6},{5,3},{6,0},{7,5},{8,10},{9,15},{10,... | collective-permute-start | bytes 786440 | tf_op jit(solution)/shard_map/ppermute | solution.py:375
  3.5 13.4 %collective-permute-start.1 = (bf16[32,4096]{1,0:T(8,128)(2,1)}, bf16[32,4096]{1,0:T(8,128)(2,1)S(1)}, u32[]{:S(2)}, u32[]{:S(2)}) collective-permute-start(bf16[32,4096]{1,0:T(8,128)(2,1)} %refs_0_.1), channel_id=1, source_target_pairs={{0,6},{1,3},{2,0},{3,5},{4,2},{5,7},{6,4},{7,1},{8,14},{9,11},{10,... | collective-permute-start | bytes 786440 | tf_op jit(solution)/shard_map/ppermute | solution.py:375
  7.1 11.3 %collective-permute-start = (bf16[32,4096]{1,0:T(8,128)(2,1)}, bf16[32,4096]{1,0:T(8,128)(2,1)}, u32[]{:S(2)}, u32[]{:S(2)}) collective-permute-start(bf16[32,4096]{1,0:T(8,128)(2,1)} %refs_0_.1), channel_id=1, source_target_pairs={{0,8},{1,9},{2,10},{3,11},{4,12},{5,13},{6,14},{7,15},{8,0},{9,1},... | collective-permute-start | bytes 786440 | tf_op jit(solution)/shard_map/ppermute | solution.py:375
  10.4 9.6 %collective-permute-start.3 = (bf16[32,4096]{1,0:T(8,128)(2,1)S(1)}, bf16[32,4096]{1,0:T(8,128)(2,1)}, u32[]{:S(2)}, u32[]{:S(2)}) collective-permute-start(bf16[32,4096]{1,0:T(8,128)(2,1)S(1)} %collective-permute-done.2.refs_1_), channel_id=1, source_target_pairs={{0,2},{1,7},{2,4},{3,1},{4,6},{5,3},{6,0},{7,5},{8,10},{9,15},{10,... | collective-permute-start | bytes 786440 | tf_op jit(solution)/shard_map/ppermute | solution.py:375
  13.0 0.8 copy-start.1
  13.9 18.1 %copy-start.6 = (s32[512]{0:T(512)S(1)}, s32[512]{0:T(512)}, u32[]{:S(2)}) copy-start(s32[512]{0:T(512)} %param.9) | copy-start | bytes 6148
  16.9 0.7 copy-start.4
  20.0 18.5 %collective-permute-start.4 = (bf16[256,4096]{1,0:T(8,128)(2,1)}, bf16[256,4096]{1,0:T(8,128)(2,1)}, u32[]{:S(2)}, u32[]{:S(2)}) collective-permute-start(bf16[256,4096]{1,0:T(8,128)(2,1)} %wave.1), channel_id=1, source_target_pairs={{0,1},{1,0},{2,3},{3,2},{4,5},{5,4},{6,7},{7,6},{8,9},{9,8},{10,11... | collective-permute-start | bytes 6291464 | tf_op jit(solution)/shard_map/ppermute | solution.py:375
  21.9 12.8 %collective-permute-start.7 = (bf16[32,4096]{1,0:T(8,128)(2,1)}, bf16[32,4096]{1,0:T(8,128)(2,1)}, u32[]{:S(2)}, u32[]{:S(2)}) collective-permute-start(bf16[32,4096]{1,0:T(8,128)(2,1)} %collective-permute-done.3.refs_3_), channel_id=1, source_target_pairs={{0,8},{1,9},{2,10},{3,11},{4,12},{5,13},{6,14},{7,15},{8,0},{9,1},... | collective-permute-start | bytes 786440 | tf_op jit(solution)/shard_map/ppermute | solution.py:375
  25.9 10.2 %collective-permute-start.6 = (bf16[32,4096]{1,0:T(8,128)(2,1)}, bf16[32,4096]{1,0:T(8,128)(2,1)}, u32[]{:S(2)}, u32[]{:S(2)}) collective-permute-start(bf16[32,4096]{1,0:T(8,128)(2,1)} %collective-permute-done.refs_4_), channel_id=1, source_target_pairs={{0,6},{1,3},{2,0},{3,5},{4,2},{5,7},{6,4},{7,1},{8,14},{9,11},{10,... | collective-permute-start | bytes 786440 | tf_op jit(solution)/shard_map/ppermute | solution.py:375
  28.7 9.8 %collective-permute-start.5 = (bf16[32,4096]{1,0:T(8,128)(2,1)}, bf16[32,4096]{1,0:T(8,128)(2,1)}, u32[]{:S(2)}, u32[]{:S(2)}) collective-permute-start(bf16[32,4096]{1,0:T(8,128)(2,1)} %collective-permute-done.refs_4_), channel_id=1, source_target_pairs={{0,2},{1,7},{2,4},{3,1},{4,6},{5,3},{6,0},{7,5},{8,10},{9,15},{10,... | collective-permute-start | bytes 786440 | tf_op jit(solution)/shard_map/ppermute | solution.py:375
  31.9 6.6 %copy-start.3 = (bf16[32,4096]{1,0:T(8,128)(2,1)S(1)}, bf16[32,4096]{1,0:T(8,128)(2,1)}, u32[]{:S(2)}) copy-start(bf16[32,4096]{1,0:T(8,128)(2,1)} %refs_0_.1) | copy-start | bytes 786436
  31.9 6.6 %copy-start.5 = (bf16[32,4096]{1,0:T(8,128)(2,1)S(1)}, bf16[32,4096]{1,0:T(8,128)(2,1)}, u32[]{:S(2)}) copy-start(bf16[32,4096]{1,0:T(8,128)(2,1)} %copy-done.4) | copy-start | bytes 786436
  41.9 0.7 copy-start
  42.6 60.5 %copy-start.2 = (s32[3,4096]{1,0:T(4,128)S(1)}, s32[3,4096]{1,0:T(4,128)}, u32[]{:S(2)}) copy-start(s32[3,4096]{1,0:T(4,128)} %gvec.3) | copy-start | bytes 147460
  42.6 16.7 %all-to-all-start = ((bf16[8,72,256]{2,1,0:T(8,128)(2,1)}), bf16[8,72,256]{2,1,0:T(8,128)(2,1)S(1)}, u32[]{:S(2)}, u32[]{:S(2)}) async-start(bf16[8,72,256]{2,1,0:T(8,128)(2,1)} %bitcast.20), calls=%async_computation | async-start | bytes 589824 | tf_op jit(solution)/shard_map/all_to_all | solution.py:396
  50.2 44.3 %collective-permute-start.8 = (bf16[256,4096]{1,0:T(8,128)(2,1)}, bf16[256,4096]{1,0:T(8,128)(2,1)}, u32[]{:S(2)}, u32[]{:S(2)}) collective-permute-start(bf16[256,4096]{1,0:T(8,128)(2,1)} %get-tuple-element.32.whole_own), channel_id=1, source_target_pairs={{0,1},{1,0},{2,3},{3,2},{4,5},{5,4},{6,7},{7,6},{8,9},{9,8},{10,11... | collective-permute-start | bytes 6291464 | tf_op jit(solution)/shard_map/ppermute | solution.py:375
  89.2 14.0 %all-to-all-start.2 = ((bf16[8,72,256]{2,1,0:T(8,128)(2,1)}), bf16[8,72,256]{2,1,0:T(8,128)(2,1)S(1)}, u32[]{:S(2)}, u32[]{:S(2)}) async-start(bf16[8,72,256]{2,1,0:T(8,128)(2,1)} %bitcast.15), calls=%async_computation.2 | async-start | bytes 589824 | tf_op jit(solution)/shard_map/all_to_all | solution.py:396

commit v5 on v3

--- a/solution.py
+++ b/solution.py
@@ -422,10 +422,10 @@
     before, after = ring(projector), against_ring(projector)
     far = ring(before)
     stat, wave_v = stats(wave, gvec)
-    across, after, far, own_wave, stat, late_dion = lax.optimization_barrier((across, after, far, wave, stat, dion))
+    wave_other = swap(wave)
+    across, after, far, stat, late_dion = lax.optimization_barrier((across, after, far, stat, dion))
     far_x = to_other_x(far)
     before_x, after_x = ring(across), against_ring(across)
-    wave_other = swap(own_wave)
     shards = [projector, before, after, far, across, before_x, after_x, far_x]
     weights = masked_weights(atom_of, late_dion, qaug)
     stat, weights = lax.optimization_barrier((stat, weights))

time: 110 us -> 110 us (level)
    all_to_all x2, waiting for transfers between devices: 15.9 us -> 14.6 us  [near_exchange(): lax.all_to_all(value, 'coef', 0, 0, axis_index_groups=groups, tiled=True)]
where the time goes in v5:
time: 110 us; the launch traced here: 109 us
  starting transfers between devices  39.5 us (36%)
  blocking collectives  28.3 us (26%)
  waiting for transfers between devices  21.1 us (19%)
  Pallas kernels  17.5 us (16%)
  local copies, waits for them, and re-layouts  2.35 us (2%)
    all_to_all x1, blocking collectives, far_exchange(): lax.all_to_all(value, ('coef', 'band'), 0, 0, axis_index_groups=groups, t...  28.3 us
    ppermute x9, starting transfers between devices, along_band(): return lax.ppermute(value, 'band', band_perm(move))  26.3 us
    all_to_all x2, waiting for transfers between devices, near_exchange(): lax.all_to_all(value, 'coef', 0, 0, axis_index_groups=groups, tiled=True)  14.6 us
    all_to_all x2, starting transfers between devices, near_exchange(): lax.all_to_all(value, 'coef', 0, 0, axis_index_groups=groups, tiled=True)  13.1 us
    ppermute x9, waiting for transfers between devices, along_band(): return lax.ppermute(value, 'band', band_perm(move))  6.53 us
    pallas_call x1, Pallas kernels, finish(): pl.pallas_call(finish_kernel, in_specs=[smem] + [vmem] * 3 + [anywhere] *...  5.8 us
    pallas_call x1, Pallas kernels, intersect(): pl.pallas_call(intersect_kernel, in_specs=[smem] + [vmem] * (3 + N_SHARDS...  3.36 us
    pallas_call x1, Pallas kernels, stats(): pl.pallas_call(stats_kernel, in_specs=[anywhere, vmem], out_specs=[vmem,...  3.04 us
  transfers between devices with their start and end apart: 11, of which 6 were waited for; matrix products, arithmetic and copies ran while one was open for 0% of the time, Pallas kernels for 8%

profile of v5, /device:TPU:6, one launch (start us, length us, event | category | flops | bytes accessed | tf_op | source)
XLA Modules:
  0.0 108.9 jit_solution(10357390336626793706)
XLA Ops:
  0.0 1.9 %collective-permute-start.4 = (bf16[256,4096]{1,0:T(8,128)(2,1)}, bf16[256,4096]{1,0:T(8,128)(2,1)}, u32[]{:S(2)}, u32[]{:S(2)}) collective-permute-start(bf16[256,4096]{1,0:T(8,128)(2,1)} %wave.1), channel_id=1, source_target_pairs={{0,1},{1,0},{2,3},{3,2},{4,5},{5,4},{6,7},{7,6},{8,9},{9,8},{10,11... | collective-permute-start | bytes 6291464 | tf_op jit(solution)/shard_map/ppermute | solution.py:382
  1.9 3.5 %collective-permute-start.2 = (bf16[32,4096]{1,0:T(8,128)(2,1)}, bf16[32,4096]{1,0:T(8,128)(2,1)S(1)}, u32[]{:S(2)}, u32[]{:S(2)}) collective-permute-start(bf16[32,4096]{1,0:T(8,128)(2,1)} %refs_0_.1), channel_id=1, source_target_pairs={{0,2},{1,7},{2,4},{3,1},{4,6},{5,3},{6,0},{7,5},{8,10},{9,15},{10,... | collective-permute-start | bytes 786440 | tf_op jit(solution)/shard_map/ppermute | solution.py:382
  5.4 3.6 %collective-permute-start.1 = (bf16[32,4096]{1,0:T(8,128)(2,1)}, bf16[32,4096]{1,0:T(8,128)(2,1)S(1)}, u32[]{:S(2)}, u32[]{:S(2)}) collective-permute-start(bf16[32,4096]{1,0:T(8,128)(2,1)} %refs_0_.1), channel_id=1, source_target_pairs={{0,6},{1,3},{2,0},{3,5},{4,2},{5,7},{6,4},{7,1},{8,14},{9,11},{10,... | collective-permute-start | bytes 786440 | tf_op jit(solution)/shard_map/ppermute | solution.py:382
  9.0 3.3 %collective-permute-start = (bf16[32,4096]{1,0:T(8,128)(2,1)}, bf16[32,4096]{1,0:T(8,128)(2,1)}, u32[]{:S(2)}, u32[]{:S(2)}) collective-permute-start(bf16[32,4096]{1,0:T(8,128)(2,1)} %refs_0_.1), channel_id=1, source_target_pairs={{0,8},{1,9},{2,10},{3,11},{4,12},{5,13},{6,14},{7,15},{8,0},{9,1},... | collective-permute-start | bytes 786440 | tf_op jit(solution)/shard_map/ppermute | solution.py:382
  12.3 0.0 collective-permute-done.2.refs_1_
  12.3 2.3 %collective-permute-start.3 = (bf16[32,4096]{1,0:T(8,128)(2,1)S(1)}, bf16[32,4096]{1,0:T(8,128)(2,1)}, u32[]{:S(2)}, u32[]{:S(2)}) collective-permute-start(bf16[32,4096]{1,0:T(8,128)(2,1)S(1)} %collective-permute-done.2.refs_1_), channel_id=1, source_target_pairs={{0,2},{1,7},{2,4},{3,1},{4,6},{5,3},{6,0},{7,5},{8,10},{9,15},{10,... | collective-permute-start | bytes 786440 | tf_op jit(solution)/shard_map/ppermute | solution.py:382
  14.6 0.0 copy-start.1
  14.6 0.8 copy-done.1
  15.5 0.0 copy-start.6
  15.5 3.0 %stats.1 = (f32[64,256]{1,0:T(8,128)S(1)}, bf16[256,4096]{1,0:T(8,128)(2,1)S(1)}) custom-call(bf16[256,4096]{1,0:T(8,128)(2,1)} %wave.1, s32[3,4096]{1,0:T(4,128)S(1)} %copy-done.1), custom_call_target="tpu_custom_call" | custom-call | flops 5242880 | bytes 2097152 | tf_op jit(solution)/shard_map/stats/pallas_call | solution.py:118
  18.5 0.0 collective-permute-done.1.refs_2_
  18.5 0.0 copy-start.4
  18.5 0.7 copy-done.4
  19.2 1.7 %collective-permute-done.refs_4_ = bf16[32,4096]{1,0:T(8,128)(2,1)} collective-permute-done((bf16[32,4096]{1,0:T(8,128)(2,1)}, bf16[32,4096]{1,0:T(8,128)(2,1)}, u32[]{:S(2)}, u32[]{:S(2)}) %collective-permute-start) | collective-permute-done | bytes 262176 | tf_op jit(solution)/shard_map/ppermute | solution.py:382
  20.9 1.0 collective-permute-done.3.refs_3_
  21.9 4.0 %collective-permute-start.7 = (bf16[32,4096]{1,0:T(8,128)(2,1)}, bf16[32,4096]{1,0:T(8,128)(2,1)}, u32[]{:S(2)}, u32[]{:S(2)}) collective-permute-start(bf16[32,4096]{1,0:T(8,128)(2,1)} %collective-permute-done.3.refs_3_), channel_id=1, source_target_pairs={{0,8},{1,9},{2,10},{3,11},{4,12},{5,13},{6,14},{7,15},{8,0},{9,1},... | collective-permute-start | bytes 786440 | tf_op jit(solution)/shard_map/ppermute | solution.py:382
  25.9 2.8 %collective-permute-start.6 = (bf16[32,4096]{1,0:T(8,128)(2,1)}, bf16[32,4096]{1,0:T(8,128)(2,1)}, u32[]{:S(2)}, u32[]{:S(2)}) collective-permute-start(bf16[32,4096]{1,0:T(8,128)(2,1)} %collective-permute-done.refs_4_), channel_id=1, source_target_pairs={{0,6},{1,3},{2,0},{3,5},{4,2},{5,7},{6,4},{7,1},{8,14},{9,11},{10,... | collective-permute-start | bytes 786440 | tf_op jit(solution)/shard_map/ppermute | solution.py:382
  28.7 3.0 %collective-permute-start.5 = (bf16[32,4096]{1,0:T(8,128)(2,1)}, bf16[32,4096]{1,0:T(8,128)(2,1)}, u32[]{:S(2)}, u32[]{:S(2)}) collective-permute-start(bf16[32,4096]{1,0:T(8,128)(2,1)} %collective-permute-done.refs_4_), channel_id=1, source_target_pairs={{0,2},{1,7},{2,4},{3,1},{4,6},{5,3},{6,0},{7,5},{8,10},{9,15},{10,... | collective-permute-start | bytes 786440 | tf_op jit(solution)/shard_map/ppermute | solution.py:382
  31.8 0.1 stack.43.place
  31.9 0.0 copy-done.6
  31.9 0.0 copy-start.3
  31.9 0.0 copy-start.5
  31.9 2.8 %masked_weights.1.weights = bf16[512,1024]{1,0:T(8,128)(2,1)S(1)} custom-call(s32[1,512]{1,0:T(1,128)S(1)} %bitcast.22, bf16[512,512]{1,0:T(8,128)(2,1)} %dion, bf16[512,512]{1,0:T(8,128)(2,1)} %qaug.1), custom_call_target="tpu_custom_call" | custom-call | flops 1207959552 | bytes 2097152 | tf_op jit(solution)/shard_map/masked_weights/pallas_call | solution.py:148
  34.7 0.0 collective-permute-done.7.refs_7_
  34.7 2.6 %collective-permute-done.6.refs_6_ = bf16[32,4096]{1,0:T(8,128)(2,1)} collective-permute-done((bf16[32,4096]{1,0:T(8,128)(2,1)}, bf16[32,4096]{1,0:T(8,128)(2,1)}, u32[]{:S(2)}, u32[]{:S(2)}) %collective-permute-start.6) | collective-permute-done | bytes 262176 | tf_op jit(solution)/shard_map/ppermute | solution.py:382
  37.3 1.2 %collective-permute-done.5.refs_5_ = bf16[32,4096]{1,0:T(8,128)(2,1)} collective-permute-done((bf16[32,4096]{1,0:T(8,128)(2,1)}, bf16[32,4096]{1,0:T(8,128)(2,1)}, u32[]{:S(2)}, u32[]{:S(2)}) %collective-permute-start.5) | collective-permute-done | bytes 262176 | tf_op jit(solution)/shard_map/ppermute | solution.py:382
  38.5 0.0 collective-permute-done.4.wave_other
  38.5 0.0 copy-done.3
  38.5 0.0 copy-done.5
  38.5 3.4 %intersect.1 = (bf16[576,256]{1,0:T(8,128)(2,1)S(1)}, bf16[256,4096]{1,0:T(8,128)(2,1)}) custom-call(s32[10]{0:T(128)S(1)} %stack.43.place, f32[64,256]{1,0:T(8,128)S(1)} %get-tuple-element.21.stat, bf16[256,4096]{1,0:T(8,128)(2,1)S(1)} %get-tuple-element.22.wave_own.wave, bf16[256,4096]{1,0:T(8,128)(2,1)} %collective-permute-done.4.wave_other, ...), custom_call_target="tpu_custom_call" | custom-call | flops 1073741824 | bytes 8388608 | tf_op jit(solution)/shard_map/intersect/pallas_call | solution.py:187
  41.9 0.0 copy-start
  41.9 0.7 copy-done
  42.6 0.0 copy-start.2
  42.6 7.9 %all-to-all-start = ((bf16[8,72,256]{2,1,0:T(8,128)(2,1)}), bf16[8,72,256]{2,1,0:T(8,128)(2,1)S(1)}, u32[]{:S(2)}, u32[]{:S(2)}) async-start(bf16[8,72,256]{2,1,0:T(8,128)(2,1)} %bitcast.20), calls=%async_computation | async-start | bytes 589824 | tf_op jit(solution)/shard_map/all_to_all | solution.py:403
  50.5 1.9 %collective-permute-start.8 = (bf16[256,4096]{1,0:T(8,128)(2,1)}, bf16[256,4096]{1,0:T(8,128)(2,1)}, u32[]{:S(2)}, u32[]{:S(2)}) collective-permute-start(bf16[256,4096]{1,0:T(8,128)(2,1)} %get-tuple-element.30.whole_own), channel_id=1, source_target_pairs={{0,1},{1,0},{2,3},{3,2},{4,5},{5,4},{6,7},{7,6},{8,9},{9,8},{10,11... | collective-permute-start | bytes 6291464 | tf_op jit(solution)/shard_map/ppermute | solution.py:382
  52.4 5.9 %all-to-all-done = bf16[8,72,256]{2,1,0:T(8,128)(2,1)S(1)} async-done(((bf16[8,72,256]{2,1,0:T(8,128)(2,1)}), bf16[8,72,256]{2,1,0:T(8,128)(2,1)S(1)}, u32[]{:S(2)}, u32[]{:S(2)}) %all-to-all-start) | async-done | bytes 294944 | tf_op jit(solution)/shard_map/all_to_all | solution.py:403
  58.3 0.7 near_sum.1
  59.1 28.3 %all_to_all.33 = bf16[8,40,256]{2,1,0:T(8,128)(2,1)S(1)} all-to-all(bf16[8,40,256]{2,1,0:T(8,128)(2,1)S(1)} %bitcast.21), channel_id=1, replica_groups={{0,1,128,129,256,257,384,385},{2,3,130,131,258,259,386,387},{4,5,132,13..., dimensions={0} | all-to-all | bytes 327680 | tf_op jit(solution)/shard_map/all_to_all | solution.py:411
  87.4 1.8 %couple.1 = bf16[576,256]{1,0:T(8,128)(2,1)} custom-call(s32[10]{0:T(128)S(1)} %stack.43.place, f32[32,256]{1,0:T(8,128)S(1)} %get-tuple-element.27.keep, bf16[320,256]{1,0:T(8,128)(2,1)S(1)} %bitcast.19, bf16[512,1024]{1,0:T(8,128)(2,1)S(1)} %masked_weights.1.weights), custom_call_target="tpu_custom_call" | custom-call | flops 100663296 | bytes 1572864 | tf_op jit(solution)/shard_map/couple/pallas_call | solution.py:264
  89.2 5.2 %all-to-all-start.2 = ((bf16[8,72,256]{2,1,0:T(8,128)(2,1)}), bf16[8,72,256]{2,1,0:T(8,128)(2,1)S(1)}, u32[]{:S(2)}, u32[]{:S(2)}) async-start(bf16[8,72,256]{2,1,0:T(8,128)(2,1)} %bitcast.15), calls=%async_computation.2 | async-start | bytes 589824 | tf_op jit(solution)/shard_map/all_to_all | solution.py:403
  94.5 0.0 collective-permute-done.8.whole_other
  94.5 8.7 %all-to-all-done.2 = bf16[8,72,256]{2,1,0:T(8,128)(2,1)S(1)} async-done(((bf16[8,72,256]{2,1,0:T(8,128)(2,1)}), bf16[8,72,256]{2,1,0:T(8,128)(2,1)S(1)}, u32[]{:S(2)}, u32[]{:S(2)}) %all-to-all-start.2) | async-done | bytes 294944 | tf_op jit(solution)/shard_map/all_to_all | solution.py:403
  103.1 0.0 copy-done.2
  103.1 5.8 %finish.1 = bf16[256,4096]{1,0:T(8,128)(2,1)} custom-call(s32[10]{0:T(128)S(1)} %stack.43.place, bf16[576,256]{1,0:T(8,128)(2,1)S(1)} %bitcast.17, s32[3,4096]{1,0:T(4,128)S(1)} %copy-done.2, bf16[256,4096]{1,0:T(8,128)(2,1)S(1)} %get-tuple-element.22.wave_own.wave, bf16[256,4096]{1,0:T(8,128)(2,1)} %get-tuple-element.30.whole_own, ...), custom_call_target="tpu_custom_call" | custom-call | flops 1073741824 | bytes 8388608 | tf_op jit(solution)/shard_map/finish/pallas_call | solution.py:359
Async XLA Ops:
  0.0 38.5 %collective-permute-start.4 = (bf16[256,4096]{1,0:T(8,128)(2,1)}, bf16[256,4096]{1,0:T(8,128)(2,1)}, u32[]{:S(2)}, u32[]{:S(2)}) collective-permute-start(bf16[256,4096]{1,0:T(8,128)(2,1)} %wave.1), channel_id=1, source_target_pairs={{0,1},{1,0},{2,3},{3,2},{4,5},{5,4},{6,7},{7,6},{8,9},{9,8},{10,11... | collective-permute-start | bytes 6291464 | tf_op jit(solution)/shard_map/ppermute | solution.py:382
  1.9 10.4 %collective-permute-start.2 = (bf16[32,4096]{1,0:T(8,128)(2,1)}, bf16[32,4096]{1,0:T(8,128)(2,1)S(1)}, u32[]{:S(2)}, u32[]{:S(2)}) collective-permute-start(bf16[32,4096]{1,0:T(8,128)(2,1)} %refs_0_.1), channel_id=1, source_target_pairs={{0,2},{1,7},{2,4},{3,1},{4,6},{5,3},{6,0},{7,5},{8,10},{9,15},{10,... | collective-permute-start | bytes 786440 | tf_op jit(solution)/shard_map/ppermute | solution.py:382
  5.4 13.1 %collective-permute-start.1 = (bf16[32,4096]{1,0:T(8,128)(2,1)}, bf16[32,4096]{1,0:T(8,128)(2,1)S(1)}, u32[]{:S(2)}, u32[]{:S(2)}) collective-permute-start(bf16[32,4096]{1,0:T(8,128)(2,1)} %refs_0_.1), channel_id=1, source_target_pairs={{0,6},{1,3},{2,0},{3,5},{4,2},{5,7},{6,4},{7,1},{8,14},{9,11},{10,... | collective-permute-start | bytes 786440 | tf_op jit(solution)/shard_map/ppermute | solution.py:382
  9.0 11.9 %collective-permute-start = (bf16[32,4096]{1,0:T(8,128)(2,1)}, bf16[32,4096]{1,0:T(8,128)(2,1)}, u32[]{:S(2)}, u32[]{:S(2)}) collective-permute-start(bf16[32,4096]{1,0:T(8,128)(2,1)} %refs_0_.1), channel_id=1, source_target_pairs={{0,8},{1,9},{2,10},{3,11},{4,12},{5,13},{6,14},{7,15},{8,0},{9,1},... | collective-permute-start | bytes 786440 | tf_op jit(solution)/shard_map/ppermute | solution.py:382
  12.3 9.6 %collective-permute-start.3 = (bf16[32,4096]{1,0:T(8,128)(2,1)S(1)}, bf16[32,4096]{1,0:T(8,128)(2,1)}, u32[]{:S(2)}, u32[]{:S(2)}) collective-permute-start(bf16[32,4096]{1,0:T(8,128)(2,1)S(1)} %collective-permute-done.2.refs_1_), channel_id=1, source_target_pairs={{0,2},{1,7},{2,4},{3,1},{4,6},{5,3},{6,0},{7,5},{8,10},{9,15},{10,... | collective-permute-start | bytes 786440 | tf_op jit(solution)/shard_map/ppermute | solution.py:382
  14.6 0.8 copy-start.1
  15.5 16.5 %copy-start.6 = (s32[512]{0:T(512)S(1)}, s32[512]{0:T(512)}, u32[]{:S(2)}) copy-start(s32[512]{0:T(512)} %param.9) | copy-start | bytes 6148
  18.5 0.7 copy-start.4
  21.9 12.8 %collective-permute-start.7 = (bf16[32,4096]{1,0:T(8,128)(2,1)}, bf16[32,4096]{1,0:T(8,128)(2,1)}, u32[]{:S(2)}, u32[]{:S(2)}) collective-permute-start(bf16[32,4096]{1,0:T(8,128)(2,1)} %collective-permute-done.3.refs_3_), channel_id=1, source_target_pairs={{0,8},{1,9},{2,10},{3,11},{4,12},{5,13},{6,14},{7,15},{8,0},{9,1},... | collective-permute-start | bytes 786440 | tf_op jit(solution)/shard_map/ppermute | solution.py:382
  25.9 11.4 %collective-permute-start.6 = (bf16[32,4096]{1,0:T(8,128)(2,1)}, bf16[32,4096]{1,0:T(8,128)(2,1)}, u32[]{:S(2)}, u32[]{:S(2)}) collective-permute-start(bf16[32,4096]{1,0:T(8,128)(2,1)} %collective-permute-done.refs_4_), channel_id=1, source_target_pairs={{0,6},{1,3},{2,0},{3,5},{4,2},{5,7},{6,4},{7,1},{8,14},{9,11},{10,... | collective-permute-start | bytes 786440 | tf_op jit(solution)/shard_map/ppermute | solution.py:382
  28.7 9.8 %collective-permute-start.5 = (bf16[32,4096]{1,0:T(8,128)(2,1)}, bf16[32,4096]{1,0:T(8,128)(2,1)}, u32[]{:S(2)}, u32[]{:S(2)}) collective-permute-start(bf16[32,4096]{1,0:T(8,128)(2,1)} %collective-permute-done.refs_4_), channel_id=1, source_target_pairs={{0,2},{1,7},{2,4},{3,1},{4,6},{5,3},{6,0},{7,5},{8,10},{9,15},{10,... | collective-permute-start | bytes 786440 | tf_op jit(solution)/shard_map/ppermute | solution.py:382
  31.9 6.6 %copy-start.3 = (bf16[32,4096]{1,0:T(8,128)(2,1)S(1)}, bf16[32,4096]{1,0:T(8,128)(2,1)}, u32[]{:S(2)}) copy-start(bf16[32,4096]{1,0:T(8,128)(2,1)} %refs_0_.1) | copy-start | bytes 786436
  31.9 6.6 %copy-start.5 = (bf16[32,4096]{1,0:T(8,128)(2,1)S(1)}, bf16[32,4096]{1,0:T(8,128)(2,1)}, u32[]{:S(2)}) copy-start(bf16[32,4096]{1,0:T(8,128)(2,1)} %copy-done.4) | copy-start | bytes 786436
  41.9 0.7 copy-start
  42.6 60.5 %copy-start.2 = (s32[3,4096]{1,0:T(4,128)S(1)}, s32[3,4096]{1,0:T(4,128)}, u32[]{:S(2)}) copy-start(s32[3,4096]{1,0:T(4,128)} %gvec.3) | copy-start | bytes 147460
  42.6 15.7 %all-to-all-start = ((bf16[8,72,256]{2,1,0:T(8,128)(2,1)}), bf16[8,72,256]{2,1,0:T(8,128)(2,1)S(1)}, u32[]{:S(2)}, u32[]{:S(2)}) async-start(bf16[8,72,256]{2,1,0:T(8,128)(2,1)} %bitcast.20), calls=%async_computation | async-start | bytes 589824 | tf_op jit(solution)/shard_map/all_to_all | solution.py:403
  50.5 43.9 %collective-permute-start.8 = (bf16[256,4096]{1,0:T(8,128)(2,1)}, bf16[256,4096]{1,0:T(8,128)(2,1)}, u32[]{:S(2)}, u32[]{:S(2)}) collective-permute-start(bf16[256,4096]{1,0:T(8,128)(2,1)} %get-tuple-element.30.whole_own), channel_id=1, source_target_pairs={{0,1},{1,0},{2,3},{3,2},{4,5},{5,4},{6,7},{7,6},{8,9},{9,8},{10,11... | collective-permute-start | bytes 6291464 | tf_op jit(solution)/shard_map/ppermute | solution.py:382
  89.2 13.9 %all-to-all-start.2 = ((bf16[8,72,256]{2,1,0:T(8,128)(2,1)}), bf16[8,72,256]{2,1,0:T(8,128)(2,1)S(1)}, u32[]{:S(2)}, u32[]{:S(2)}) async-start(bf16[8,72,256]{2,1,0:T(8,128)(2,1)} %bitcast.15), calls=%async_computation.2 | async-start | bytes 589824 | tf_op jit(solution)/shard_map/all_to_all | solution.py:403

commit v6 on v3

--- a/solution.py
+++ b/solution.py
@@ -273,6 +273,7 @@
 
 
 TILE = 512
+PART = 256
 N_TILES = COLS // TILE
 CHUNK = 16
 
@@ -303,18 +304,20 @@
         expanded_v[...] = jnp.dot(halves_v[...], whole_v[:, cols], preferred_element_type=f32)
 
     def conclude(tile, expanded_v):
-        cols = columns(tile)
-        kin = jnp.broadcast_to(kinetic(gvec[:, cols]), (CHUNK, TILE))
-        for i in range(ROWS // CHUNK):
-            rows = slice(i * CHUNK, (i + 1) * CHUNK)
-            energy = jnp.concatenate([energy_v[rows, :]] * (TILE // 128), axis=1)
-            scale = jnp.concatenate([scale_v[rows, :]] * (TILE // 128), axis=1)
-            resid = (kin - energy) * wave[rows, cols].astype(f32) + expanded_v[rows, :]
-            t = kin * scale
-            square = t * t
-            num = (3.0 + t) * (9.0 + square)
-            inverse = pl.reciprocal(num + square * square, approx=True)
-            out_v[rows, cols] = ((num * inverse) * resid).astype(bf16)
+        for part in range(TILE // PART):
+            cols = pl.ds(pl.multiple_of(tile * TILE + part * PART, PART), PART)
+            kin = jnp.broadcast_to(kinetic(gvec[:, cols]), (CHUNK, PART))
+            for i in range(ROWS // CHUNK):
+                rows = slice(i * CHUNK, (i + 1) * CHUNK)
+                energy = jnp.concatenate([energy_v[rows, :]] * (PART // 128), axis=1)
+                scale = jnp.concatenate([scale_v[rows, :]] * (PART // 128), axis=1)
+                expanded = expanded_v[rows, part * PART:(part + 1) * PART]
+                resid = (kin - energy) * wave[rows, cols].astype(f32) + expanded
+                t = kin * scale
+                square = t * t
+                num = (3.0 + t) * (9.0 + square)
+                inverse = pl.reciprocal(num + square * square, approx=True)
+                out_v[rows, cols] = ((num * inverse) * resid).astype(bf16)
 
     def depart(tiles):
         for tile in tiles:

time: 110 us -> 110 us (level)
  no operation moved by 1% of the time
where the time goes in v6:
time: 110 us; the launch traced here: 109 us
  starting transfers between devices  39.5 us (36%)
  blocking collectives  27.3 us (25%)
  waiting for transfers between devices  22 us (20%)
  Pallas kernels  17.5 us (16%)
  local copies, waits for them, and re-layouts  2.35 us (2%)
    all_to_all x1, blocking collectives, far_exchange(): lax.all_to_all(value, ('coef', 'band'), 0, 0, axis_index_groups=groups, t...  27.3 us
    ppermute x9, starting transfers between devices, along_band(): return lax.ppermute(value, 'band', band_perm(move))  26.7 us
    all_to_all x2, waiting for transfers between devices, near_exchange(): lax.all_to_all(value, 'coef', 0, 0, axis_index_groups=groups, tiled=True)  15.9 us
    all_to_all x2, starting transfers between devices, near_exchange(): lax.all_to_all(value, 'coef', 0, 0, axis_index_groups=groups, tiled=True)  12.9 us
    ppermute x9, waiting for transfers between devices, along_band(): return lax.ppermute(value, 'band', band_perm(move))  6.16 us
    pallas_call x1, Pallas kernels, finish(): pl.pallas_call(finish_kernel, in_specs=[smem] + [vmem] * 3 + [anywhere] *...  5.82 us
    pallas_call x1, Pallas kernels, intersect(): pl.pallas_call(intersect_kernel, in_specs=[smem] + [vmem] * (3 + N_SHARDS...  3.36 us
    pallas_call x1, Pallas kernels, stats(): pl.pallas_call(stats_kernel, in_specs=[anywhere, vmem], out_specs=[vmem,...  3.04 us
  transfers between devices with their start and end apart: 11, of which 6 were waited for; matrix products, arithmetic and copies ran while one was open for 0% of the time, Pallas kernels for 8%

profile of v6, /device:TPU:6, one launch (start us, length us, event | category | flops | bytes accessed | tf_op | source)
XLA Modules:
  0.0 109.0 jit_solution(9465303667388033660)
XLA Ops:
  0.0 3.5 %collective-permute-start.2 = (bf16[32,4096]{1,0:T(8,128)(2,1)}, bf16[32,4096]{1,0:T(8,128)(2,1)S(1)}, u32[]{:S(2)}, u32[]{:S(2)}) collective-permute-start(bf16[32,4096]{1,0:T(8,128)(2,1)} %refs_0_.1), channel_id=1, source_target_pairs={{0,2},{1,7},{2,4},{3,1},{4,6},{5,3},{6,0},{7,5},{8,10},{9,15},{10,... | collective-permute-start | bytes 786440 | tf_op jit(solution)/shard_map/ppermute | solution.py:385
  3.5 3.6 %collective-permute-start.1 = (bf16[32,4096]{1,0:T(8,128)(2,1)}, bf16[32,4096]{1,0:T(8,128)(2,1)S(1)}, u32[]{:S(2)}, u32[]{:S(2)}) collective-permute-start(bf16[32,4096]{1,0:T(8,128)(2,1)} %refs_0_.1), channel_id=1, source_target_pairs={{0,6},{1,3},{2,0},{3,5},{4,2},{5,7},{6,4},{7,1},{8,14},{9,11},{10,... | collective-permute-start | bytes 786440 | tf_op jit(solution)/shard_map/ppermute | solution.py:385
  7.1 3.3 %collective-permute-start = (bf16[32,4096]{1,0:T(8,128)(2,1)}, bf16[32,4096]{1,0:T(8,128)(2,1)}, u32[]{:S(2)}, u32[]{:S(2)}) collective-permute-start(bf16[32,4096]{1,0:T(8,128)(2,1)} %refs_0_.1), channel_id=1, source_target_pairs={{0,8},{1,9},{2,10},{3,11},{4,12},{5,13},{6,14},{7,15},{8,0},{9,1},... | collective-permute-start | bytes 786440 | tf_op jit(solution)/shard_map/ppermute | solution.py:385
  10.4 0.0 collective-permute-done.2.refs_1_
  10.4 2.6 %collective-permute-start.3 = (bf16[32,4096]{1,0:T(8,128)(2,1)S(1)}, bf16[32,4096]{1,0:T(8,128)(2,1)}, u32[]{:S(2)}, u32[]{:S(2)}) collective-permute-start(bf16[32,4096]{1,0:T(8,128)(2,1)S(1)} %collective-permute-done.2.refs_1_), channel_id=1, source_target_pairs={{0,2},{1,7},{2,4},{3,1},{4,6},{5,3},{6,0},{7,5},{8,10},{9,15},{10,... | collective-permute-start | bytes 786440 | tf_op jit(solution)/shard_map/ppermute | solution.py:385
  13.0 0.0 copy-start.1
  13.0 0.8 copy-done.1
  13.9 0.0 copy-start.6
  13.9 3.0 %stats.1 = (f32[64,256]{1,0:T(8,128)S(1)}, bf16[256,4096]{1,0:T(8,128)(2,1)S(1)}) custom-call(bf16[256,4096]{1,0:T(8,128)(2,1)} %wave.1, s32[3,4096]{1,0:T(4,128)S(1)} %copy-done.1), custom_call_target="tpu_custom_call" | custom-call | flops 5242880 | bytes 2097152 | tf_op jit(solution)/shard_map/stats/pallas_call | solution.py:118
  16.9 0.0 collective-permute-done.1.refs_2_
  16.9 0.0 copy-start.4
  16.9 0.7 copy-done.4
  17.6 0.7 collective-permute-done.refs_4_
  18.3 1.6 %collective-permute-done.3.refs_3_ = bf16[32,4096]{1,0:T(8,128)(2,1)} collective-permute-done((bf16[32,4096]{1,0:T(8,128)(2,1)S(1)}, bf16[32,4096]{1,0:T(8,128)(2,1)}, u32[]{:S(2)}, u32[]{:S(2)}) %collective-permute-start.3) | collective-permute-done | bytes 262176 | tf_op jit(solution)/shard_map/ppermute | solution.py:385
  20.0 1.9 %collective-permute-start.4 = (bf16[256,4096]{1,0:T(8,128)(2,1)}, bf16[256,4096]{1,0:T(8,128)(2,1)}, u32[]{:S(2)}, u32[]{:S(2)}) collective-permute-start(bf16[256,4096]{1,0:T(8,128)(2,1)} %wave.1), channel_id=1, source_target_pairs={{0,1},{1,0},{2,3},{3,2},{4,5},{5,4},{6,7},{7,6},{8,9},{9,8},{10,11... | collective-permute-start | bytes 6291464 | tf_op jit(solution)/shard_map/ppermute | solution.py:385
  21.9 4.0 %collective-permute-start.7 = (bf16[32,4096]{1,0:T(8,128)(2,1)}, bf16[32,4096]{1,0:T(8,128)(2,1)}, u32[]{:S(2)}, u32[]{:S(2)}) collective-permute-start(bf16[32,4096]{1,0:T(8,128)(2,1)} %collective-permute-done.3.refs_3_), channel_id=1, source_target_pairs={{0,8},{1,9},{2,10},{3,11},{4,12},{5,13},{6,14},{7,15},{8,0},{9,1},... | collective-permute-start | bytes 786440 | tf_op jit(solution)/shard_map/ppermute | solution.py:385
  25.9 2.8 %collective-permute-start.6 = (bf16[32,4096]{1,0:T(8,128)(2,1)}, bf16[32,4096]{1,0:T(8,128)(2,1)}, u32[]{:S(2)}, u32[]{:S(2)}) collective-permute-start(bf16[32,4096]{1,0:T(8,128)(2,1)} %collective-permute-done.refs_4_), channel_id=1, source_target_pairs={{0,6},{1,3},{2,0},{3,5},{4,2},{5,7},{6,4},{7,1},{8,14},{9,11},{10,... | collective-permute-start | bytes 786440 | tf_op jit(solution)/shard_map/ppermute | solution.py:385
  28.7 3.1 %collective-permute-start.5 = (bf16[32,4096]{1,0:T(8,128)(2,1)}, bf16[32,4096]{1,0:T(8,128)(2,1)}, u32[]{:S(2)}, u32[]{:S(2)}) collective-permute-start(bf16[32,4096]{1,0:T(8,128)(2,1)} %collective-permute-done.refs_4_), channel_id=1, source_target_pairs={{0,2},{1,7},{2,4},{3,1},{4,6},{5,3},{6,0},{7,5},{8,10},{9,15},{10,... | collective-permute-start | bytes 786440 | tf_op jit(solution)/shard_map/ppermute | solution.py:385
  31.8 0.1 stack.43.place
  31.9 0.0 copy-done.6
  31.9 0.0 copy-start.3
  31.9 0.0 copy-start.5
  31.9 2.8 %masked_weights.1.weights = bf16[512,1024]{1,0:T(8,128)(2,1)S(1)} custom-call(s32[1,512]{1,0:T(1,128)S(1)} %bitcast.22, bf16[512,512]{1,0:T(8,128)(2,1)} %dion, bf16[512,512]{1,0:T(8,128)(2,1)} %qaug.1), custom_call_target="tpu_custom_call" | custom-call | flops 1207959552 | bytes 2097152 | tf_op jit(solution)/shard_map/masked_weights/pallas_call | solution.py:148
  34.7 0.0 collective-permute-done.7.refs_7_
  34.7 1.4 %collective-permute-done.6.refs_6_ = bf16[32,4096]{1,0:T(8,128)(2,1)} collective-permute-done((bf16[32,4096]{1,0:T(8,128)(2,1)}, bf16[32,4096]{1,0:T(8,128)(2,1)}, u32[]{:S(2)}, u32[]{:S(2)}) %collective-permute-start.6) | collective-permute-done | bytes 262176 | tf_op jit(solution)/shard_map/ppermute | solution.py:385
  36.1 2.4 %collective-permute-done.5.refs_5_ = bf16[32,4096]{1,0:T(8,128)(2,1)} collective-permute-done((bf16[32,4096]{1,0:T(8,128)(2,1)}, bf16[32,4096]{1,0:T(8,128)(2,1)}, u32[]{:S(2)}, u32[]{:S(2)}) %collective-permute-start.5) | collective-permute-done | bytes 262176 | tf_op jit(solution)/shard_map/ppermute | solution.py:385
  38.5 0.0 collective-permute-done.4.wave_other
  38.5 0.0 copy-done.3
  38.5 0.0 copy-done.5
  38.5 3.4 %intersect.1 = (bf16[576,256]{1,0:T(8,128)(2,1)S(1)}, bf16[256,4096]{1,0:T(8,128)(2,1)}) custom-call(s32[10]{0:T(128)S(1)} %stack.43.place, f32[64,256]{1,0:T(8,128)S(1)} %get-tuple-element.22.stat, bf16[256,4096]{1,0:T(8,128)(2,1)S(1)} %get-tuple-element.23.wave_own.wave, bf16[256,4096]{1,0:T(8,128)(2,1)} %collective-permute-done.4.wave_other, ...), custom_call_target="tpu_custom_call" | custom-call | flops 1073741824 | bytes 8388608 | tf_op jit(solution)/shard_map/intersect/pallas_call | solution.py:187
  41.9 0.0 copy-start
  41.9 0.7 copy-done
  42.6 0.0 copy-start.2
  42.6 7.6 %all-to-all-start = ((bf16[8,72,256]{2,1,0:T(8,128)(2,1)}), bf16[8,72,256]{2,1,0:T(8,128)(2,1)S(1)}, u32[]{:S(2)}, u32[]{:S(2)}) async-start(bf16[8,72,256]{2,1,0:T(8,128)(2,1)} %bitcast.20), calls=%async_computation | async-start | bytes 589824 | tf_op jit(solution)/shard_map/all_to_all | solution.py:406
  50.2 1.9 %collective-permute-start.8 = (bf16[256,4096]{1,0:T(8,128)(2,1)}, bf16[256,4096]{1,0:T(8,128)(2,1)}, u32[]{:S(2)}, u32[]{:S(2)}) collective-permute-start(bf16[256,4096]{1,0:T(8,128)(2,1)} %get-tuple-element.32.whole_own), channel_id=1, source_target_pairs={{0,1},{1,0},{2,3},{3,2},{4,5},{5,4},{6,7},{7,6},{8,9},{9,8},{10,11... | collective-permute-start | bytes 6291464 | tf_op jit(solution)/shard_map/ppermute | solution.py:385
  52.1 7.2 %all-to-all-done = bf16[8,72,256]{2,1,0:T(8,128)(2,1)S(1)} async-done(((bf16[8,72,256]{2,1,0:T(8,128)(2,1)}), bf16[8,72,256]{2,1,0:T(8,128)(2,1)S(1)}, u32[]{:S(2)}, u32[]{:S(2)}) %all-to-all-start) | async-done | bytes 294944 | tf_op jit(solution)/shard_map/all_to_all | solution.py:406
  59.3 0.7 near_sum.1
  60.0 27.3 %all_to_all.33 = bf16[8,40,256]{2,1,0:T(8,128)(2,1)S(1)} all-to-all(bf16[8,40,256]{2,1,0:T(8,128)(2,1)S(1)} %bitcast.21), channel_id=1, replica_groups={{0,1,128,129,256,257,384,385},{2,3,130,131,258,259,386,387},{4,5,132,13..., dimensions={0} | all-to-all | bytes 327680 | tf_op jit(solution)/shard_map/all_to_all | solution.py:414
  87.4 1.8 %couple.1 = bf16[576,256]{1,0:T(8,128)(2,1)} custom-call(s32[10]{0:T(128)S(1)} %stack.43.place, f32[32,256]{1,0:T(8,128)S(1)} %get-tuple-element.29.keep, bf16[320,256]{1,0:T(8,128)(2,1)S(1)} %bitcast.19, bf16[512,1024]{1,0:T(8,128)(2,1)S(1)} %masked_weights.1.weights), custom_call_target="tpu_custom_call" | custom-call | flops 100663296 | bytes 1572864 | tf_op jit(solution)/shard_map/couple/pallas_call | solution.py:264
  89.2 5.3 %all-to-all-start.2 = ((bf16[8,72,256]{2,1,0:T(8,128)(2,1)}), bf16[8,72,256]{2,1,0:T(8,128)(2,1)S(1)}, u32[]{:S(2)}, u32[]{:S(2)}) async-start(bf16[8,72,256]{2,1,0:T(8,128)(2,1)} %bitcast.15), calls=%async_computation.2 | async-start | bytes 589824 | tf_op jit(solution)/shard_map/all_to_all | solution.py:406
  94.5 0.0 collective-permute-done.8.whole_other
  94.5 8.7 %all-to-all-done.2 = bf16[8,72,256]{2,1,0:T(8,128)(2,1)S(1)} async-done(((bf16[8,72,256]{2,1,0:T(8,128)(2,1)}), bf16[8,72,256]{2,1,0:T(8,128)(2,1)S(1)}, u32[]{:S(2)}, u32[]{:S(2)}) %all-to-all-start.2) | async-done | bytes 294944 | tf_op jit(solution)/shard_map/all_to_all | solution.py:406
  103.1 0.0 copy-done.2
  103.1 5.8 %finish.1 = bf16[256,4096]{1,0:T(8,128)(2,1)} custom-call(s32[10]{0:T(128)S(1)} %stack.43.place, bf16[576,256]{1,0:T(8,128)(2,1)S(1)} %bitcast.17, s32[3,4096]{1,0:T(4,128)S(1)} %copy-done.2, bf16[256,4096]{1,0:T(8,128)(2,1)S(1)} %get-tuple-element.23.wave_own.wave, bf16[256,4096]{1,0:T(8,128)(2,1)} %get-tuple-element.32.whole_own, ...), custom_call_target="tpu_custom_call" | custom-call | flops 1073741824 | bytes 8388608 | tf_op jit(solution)/shard_map/finish/pallas_call | solution.py:362
Async XLA Ops:
  0.0 10.4 %collective-permute-start.2 = (bf16[32,4096]{1,0:T(8,128)(2,1)}, bf16[32,4096]{1,0:T(8,128)(2,1)S(1)}, u32[]{:S(2)}, u32[]{:S(2)}) collective-permute-start(bf16[32,4096]{1,0:T(8,128)(2,1)} %refs_0_.1), channel_id=1, source_target_pairs={{0,2},{1,7},{2,4},{3,1},{4,6},{5,3},{6,0},{7,5},{8,10},{9,15},{10,... | collective-permute-start | bytes 786440 | tf_op jit(solution)/shard_map/ppermute | solution.py:385
  3.5 13.4 %collective-permute-start.1 = (bf16[32,4096]{1,0:T(8,128)(2,1)}, bf16[32,4096]{1,0:T(8,128)(2,1)S(1)}, u32[]{:S(2)}, u32[]{:S(2)}) collective-permute-start(bf16[32,4096]{1,0:T(8,128)(2,1)} %refs_0_.1), channel_id=1, source_target_pairs={{0,6},{1,3},{2,0},{3,5},{4,2},{5,7},{6,4},{7,1},{8,14},{9,11},{10,... | collective-permute-start | bytes 786440 | tf_op jit(solution)/shard_map/ppermute | solution.py:385
  7.1 11.3 %collective-permute-start = (bf16[32,4096]{1,0:T(8,128)(2,1)}, bf16[32,4096]{1,0:T(8,128)(2,1)}, u32[]{:S(2)}, u32[]{:S(2)}) collective-permute-start(bf16[32,4096]{1,0:T(8,128)(2,1)} %refs_0_.1), channel_id=1, source_target_pairs={{0,8},{1,9},{2,10},{3,11},{4,12},{5,13},{6,14},{7,15},{8,0},{9,1},... | collective-permute-start | bytes 786440 | tf_op jit(solution)/shard_map/ppermute | solution.py:385
  10.4 9.6 %collective-permute-start.3 = (bf16[32,4096]{1,0:T(8,128)(2,1)S(1)}, bf16[32,4096]{1,0:T(8,128)(2,1)}, u32[]{:S(2)}, u32[]{:S(2)}) collective-permute-start(bf16[32,4096]{1,0:T(8,128)(2,1)S(1)} %collective-permute-done.2.refs_1_), channel_id=1, source_target_pairs={{0,2},{1,7},{2,4},{3,1},{4,6},{5,3},{6,0},{7,5},{8,10},{9,15},{10,... | collective-permute-start | bytes 786440 | tf_op jit(solution)/shard_map/ppermute | solution.py:385
  13.0 0.8 copy-start.1
  13.9 18.1 %copy-start.6 = (s32[512]{0:T(512)S(1)}, s32[512]{0:T(512)}, u32[]{:S(2)}) copy-start(s32[512]{0:T(512)} %param.9) | copy-start | bytes 6148
  16.9 0.7 copy-start.4
  20.0 18.5 %collective-permute-start.4 = (bf16[256,4096]{1,0:T(8,128)(2,1)}, bf16[256,4096]{1,0:T(8,128)(2,1)}, u32[]{:S(2)}, u32[]{:S(2)}) collective-permute-start(bf16[256,4096]{1,0:T(8,128)(2,1)} %wave.1), channel_id=1, source_target_pairs={{0,1},{1,0},{2,3},{3,2},{4,5},{5,4},{6,7},{7,6},{8,9},{9,8},{10,11... | collective-permute-start | bytes 6291464 | tf_op jit(solution)/shard_map/ppermute | solution.py:385
  21.9 12.8 %collective-permute-start.7 = (bf16[32,4096]{1,0:T(8,128)(2,1)}, bf16[32,4096]{1,0:T(8,128)(2,1)}, u32[]{:S(2)}, u32[]{:S(2)}) collective-permute-start(bf16[32,4096]{1,0:T(8,128)(2,1)} %collective-permute-done.3.refs_3_), channel_id=1, source_target_pairs={{0,8},{1,9},{2,10},{3,11},{4,12},{5,13},{6,14},{7,15},{8,0},{9,1},... | collective-permute-start | bytes 786440 | tf_op jit(solution)/shard_map/ppermute | solution.py:385
  25.9 10.2 %collective-permute-start.6 = (bf16[32,4096]{1,0:T(8,128)(2,1)}, bf16[32,4096]{1,0:T(8,128)(2,1)}, u32[]{:S(2)}, u32[]{:S(2)}) collective-permute-start(bf16[32,4096]{1,0:T(8,128)(2,1)} %collective-permute-done.refs_4_), channel_id=1, source_target_pairs={{0,6},{1,3},{2,0},{3,5},{4,2},{5,7},{6,4},{7,1},{8,14},{9,11},{10,... | collective-permute-start | bytes 786440 | tf_op jit(solution)/shard_map/ppermute | solution.py:385
  28.7 9.8 %collective-permute-start.5 = (bf16[32,4096]{1,0:T(8,128)(2,1)}, bf16[32,4096]{1,0:T(8,128)(2,1)}, u32[]{:S(2)}, u32[]{:S(2)}) collective-permute-start(bf16[32,4096]{1,0:T(8,128)(2,1)} %collective-permute-done.refs_4_), channel_id=1, source_target_pairs={{0,2},{1,7},{2,4},{3,1},{4,6},{5,3},{6,0},{7,5},{8,10},{9,15},{10,... | collective-permute-start | bytes 786440 | tf_op jit(solution)/shard_map/ppermute | solution.py:385
  31.9 6.6 %copy-start.3 = (bf16[32,4096]{1,0:T(8,128)(2,1)S(1)}, bf16[32,4096]{1,0:T(8,128)(2,1)}, u32[]{:S(2)}) copy-start(bf16[32,4096]{1,0:T(8,128)(2,1)} %refs_0_.1) | copy-start | bytes 786436
  31.9 6.6 %copy-start.5 = (bf16[32,4096]{1,0:T(8,128)(2,1)S(1)}, bf16[32,4096]{1,0:T(8,128)(2,1)}, u32[]{:S(2)}) copy-start(bf16[32,4096]{1,0:T(8,128)(2,1)} %copy-done.4) | copy-start | bytes 786436
  41.9 0.7 copy-start
  42.6 60.5 %copy-start.2 = (s32[3,4096]{1,0:T(4,128)S(1)}, s32[3,4096]{1,0:T(4,128)}, u32[]{:S(2)}) copy-start(s32[3,4096]{1,0:T(4,128)} %gvec.3) | copy-start | bytes 147460
  42.6 16.7 %all-to-all-start = ((bf16[8,72,256]{2,1,0:T(8,128)(2,1)}), bf16[8,72,256]{2,1,0:T(8,128)(2,1)S(1)}, u32[]{:S(2)}, u32[]{:S(2)}) async-start(bf16[8,72,256]{2,1,0:T(8,128)(2,1)} %bitcast.20), calls=%async_computation | async-start | bytes 589824 | tf_op jit(solution)/shard_map/all_to_all | solution.py:406
  50.2 44.3 %collective-permute-start.8 = (bf16[256,4096]{1,0:T(8,128)(2,1)}, bf16[256,4096]{1,0:T(8,128)(2,1)}, u32[]{:S(2)}, u32[]{:S(2)}) collective-permute-start(bf16[256,4096]{1,0:T(8,128)(2,1)} %get-tuple-element.32.whole_own), channel_id=1, source_target_pairs={{0,1},{1,0},{2,3},{3,2},{4,5},{5,4},{6,7},{7,6},{8,9},{9,8},{10,11... | collective-permute-start | bytes 6291464 | tf_op jit(solution)/shard_map/ppermute | solution.py:385
  89.2 14.0 %all-to-all-start.2 = ((bf16[8,72,256]{2,1,0:T(8,128)(2,1)}), bf16[8,72,256]{2,1,0:T(8,128)(2,1)S(1)}, u32[]{:S(2)}, u32[]{:S(2)}) async-start(bf16[8,72,256]{2,1,0:T(8,128)(2,1)} %bitcast.15), calls=%async_computation.2 | async-start | bytes 589824 | tf_op jit(solution)/shard_map/all_to_all | solution.py:406
